TPU v7x, 512 devices: a whole 4x4x16 slice. The times are simulated.
512 devices in a mesh: lon: 64 (over y, z_lo, core), lat: 8 (over x, z_hi).
Axes of the slice: x: 4, y: 4, z: 16 (z_hi: 2, z_lo: 8; z = z_hi * 8 + z_lo), core: 2. Of those that a mesh axis runs over, the one named last changes fastest.
Arguments:
- latent: bfloat16 [2, 48, 1536, 192], P(None, 'lat', 'lon'), may hold values from -6 to 6
- out_grad: bfloat16 [2, 48, 1536, 192], P(None, 'lat', 'lon'), may hold values from -6 to 6
- norm_gain: float32 [192], replicated, may hold values from 0.1 to 1.9
- norm_shift: float32 [192], replicated, may hold values from -3 to 3
- qkv_weight: bfloat16 [192, 576], replicated, may hold values from -0.4375 to 0.4375
- query_bias: float32 [192], replicated, may hold values from -3 to 3
- proj_weight: bfloat16 [192, 192], replicated, may hold values from -0.4375 to 0.4375
- bias_table: float32 [8, 1, 6, 3312], P('lat'), may hold values from -3 to 3
- band_rows: int32 [8], P('lat'), may hold values from 0 to 7, as said below
Outputs:
- latent_grad: bfloat16 [2, 48, 1536, 192], P(None, 'lat', 'lon')
- table_grad: float32 [8, 1, 6, 3312], P('lat')
Inputs may be any that keep to these rules, and one draw needn't show every extreme that they name: `band_rows`: in each aligned block of 1 entries, starting at 1 * k, the entries are a permutation of 1 * k to 1 * k + 1 - 1.
All inputs are finite; a program needn't handle non-finite values.
Results may differ from a plain program's by a relative error of at most 0.0099.
Values may be sent and summed in bfloat16 or wider, within the bound.
A program may use at most 128 MiB of HBM per device.

v0:
```python
import jax
import jax.numpy as jnp
from jax import lax
from jax.sharding import PartitionSpec as P

HEADS = 6
WPL = 2
WLAT = 6
WLON = 12


EPSILON = 1e-05
HIGHEST_PRECISION = lax.Precision.HIGHEST


def from_behind(array, axis, by):
    size = lax.axis_size(axis)
    return lax.ppermute(array, axis, [(i, (i + by) % size) for i in range(size)])


def as_sent(array):
    return jax.tree.map(lambda a: a.astype(jnp.bfloat16) if a.dtype == jnp.float32 else a, array)


def attention_grads(
    tokens, incoming, bias_win, allowed, norm_gain, norm_shift, qkv_weight, query_bias, proj_weight
):
    features = tokens.shape[-1]
    head_size = features // HEADS
    factor = head_size ** (-0.5)
    head_shape = tokens.shape[:-1] + (HEADS, head_size)
    values = tokens.astype(jnp.float32)
    center = jnp.mean(values, -1, keepdims=True)
    spread = jnp.mean(jnp.square(values - center), -1, keepdims=True)
    inverse = lax.rsqrt(spread + EPSILON)
    normed = (values - center) * inverse
    hidden = (normed * norm_gain + norm_shift).astype(jnp.bfloat16)
    projected = jnp.dot(hidden, qkv_weight, preferred_element_type=jnp.float32)
    queries = (projected[..., :features] + query_bias).astype(jnp.bfloat16).reshape(head_shape)
    keys_low = projected[..., features : 2 * features].astype(jnp.bfloat16).reshape(head_shape)
    vals_low = projected[..., 2 * features :].astype(jnp.bfloat16).reshape(head_shape)
    scores = (
        factor
        * jnp.einsum("...ihe,...jhe->...hij", queries, keys_low, preferred_element_type=jnp.float32)
        + bias_win
    )
    weights = jnp.where(allowed, jnp.exp(scores), 0.0)
    probabilities = weights / jnp.sum(weights, -1, keepdims=True)
    upstream = (
        jnp.dot(incoming, proj_weight.T, preferred_element_type=jnp.float32)
        .astype(jnp.bfloat16)
        .reshape(head_shape)
    )
    prob_grad = jnp.einsum(
        "...ihe,...jhe->...hij", upstream, vals_low, preferred_element_type=jnp.float32
    )
    value_grad = jnp.einsum(
        "...hij,...ihe->...jhe",
        probabilities.astype(jnp.bfloat16),
        upstream,
        preferred_element_type=jnp.float32,
    ).astype(jnp.bfloat16)
    score_grad = probabilities * (prob_grad - jnp.sum(probabilities * prob_grad, -1, keepdims=True))
    score_low = score_grad.astype(jnp.bfloat16)
    query_grad = (
        factor
        * jnp.einsum(
            "...hij,...jhe->...ihe", score_low, keys_low, preferred_element_type=jnp.float32
        )
    ).astype(jnp.bfloat16)
    key_grad = (
        factor
        * jnp.einsum(
            "...hij,...ihe->...jhe", score_low, queries, preferred_element_type=jnp.float32
        )
    ).astype(jnp.bfloat16)
    stacked = jnp.concatenate(
        [
            query_grad.reshape(tokens.shape),
            key_grad.reshape(tokens.shape),
            value_grad.reshape(tokens.shape),
        ],
        -1,
    )
    hidden_grad = jnp.dot(stacked, qkv_weight.T, preferred_element_type=jnp.float32)
    normed_grad = hidden_grad * norm_gain
    branch = inverse * (
        normed_grad
        - jnp.mean(normed_grad, -1, keepdims=True)
        - normed * jnp.mean(normed_grad * normed, -1, keepdims=True)
    )
    return (branch, score_grad)


def lat_rim(paired, half_lat):
    arrived = from_behind(paired[:, :, :half_lat], "lat", -1)
    return jnp.concatenate([paired[:, :, half_lat:], arrived], 2)


def lon_rim(paired, half_lon):
    arrived = from_behind(paired[:, :, :, :half_lon], "lon", -1)
    return jnp.concatenate([paired[:, :, :, half_lon:], arrived], 3)


def lat_return(field_grad, half_lat):
    arrived = from_behind(as_sent(field_grad[:, -half_lat:]), "lat", 1)
    return jnp.concatenate([arrived, field_grad[:, :-half_lat]], 1)


def lon_return(field_grad, half_lon):
    arrived = from_behind(field_grad[:, :, -half_lon:].astype(jnp.bfloat16), "lon", 1).astype(
        jnp.float32
    )
    return jnp.concatenate([arrived, field_grad[:, :, :-half_lon]], 2)


def table_terms(score_grad, onehot, selector):
    level_wins, lat_wins = (score_grad.shape[0], score_grad.shape[1])
    summed = jnp.sum(score_grad, axis=2)
    unfolded = summed.reshape(level_wins, lat_wins, HEADS, WPL, WLAT, WLON, WPL, WLAT, WLON)
    folded = jnp.einsum("xlhpaoqbr,dor->xlhpqabd", unfolded, onehot, precision=HIGHEST_PRECISION)
    flat_terms = folded.reshape(level_wins, lat_wins, HEADS, -1)
    return jnp.einsum("lm,xlhr->mxhr", selector, flat_terms, precision=HIGHEST_PRECISION)


def window_view(block, level_wins, lat_count, lon_count, features):
    window_size = WPL * WLAT * WLON
    shaped = block.reshape(2, level_wins, WPL, lat_count, WLAT, lon_count, WLON, features)
    return shaped.transpose(0, 1, 3, 5, 2, 4, 6, 7).reshape(
        2, level_wins, lat_count, lon_count, window_size, features
    )


def group_mask(level_wins, lat_count, levels, lat_flag):
    window_size = WPL * WLAT * WLON
    level_flag = (jnp.arange(levels) >= levels - WPL // 2).astype(jnp.int32)
    groups = level_flag[:, None] * 2 + lat_flag[None, :]
    groups = groups.reshape(level_wins, WPL, lat_count, WLAT).transpose(0, 2, 1, 3)
    groups = jnp.broadcast_to(groups[..., None], (level_wins, lat_count, WPL, WLAT, WLON)).reshape(
        level_wins, lat_count, window_size
    )
    return (groups[:, :, :, None] == groups[:, :, None, :])[:, :, None, None, :, :]


def bias_windows(chosen, onehot, level_wins):
    window_size = WPL * WLAT * WLON
    lat_count = chosen.shape[0]
    chosen = chosen.reshape(lat_count, level_wins, HEADS, WPL, WPL, WLAT, WLAT, 2 * WLON - 1)
    bias_win = jnp.einsum("lxhpqabd,dor->xlhpaoqbr", chosen, onehot, precision=HIGHEST_PRECISION)
    return bias_win.reshape(level_wins, lat_count, 1, HEADS, window_size, window_size)


def local(
    latent,
    out_grad,
    norm_gain,
    norm_shift,
    qkv_weight,
    query_bias,
    proj_weight,
    bias_table,
    band_rows,
):
    levels, lat_rows, lon_cols, features = latent.shape
    half_level = WPL // 2
    half_lat = WLAT // 2
    half_lon = WLON // 2
    level_wins = levels // WPL
    lat_wins = lat_rows // WLAT
    lon_wins = lon_cols // WLON
    lat_total = lat_rows * lax.axis_size("lat")
    paired = jnp.roll(jnp.stack([latent, out_grad]), -half_level, axis=1)
    row_base = lax.axis_index("lat") * lat_wins
    selector = (
        band_rows[:, None] - row_base == jnp.arange(lat_wins, dtype=jnp.int32)[None, :]
    ).astype(jnp.float32)
    chosen = jnp.einsum("lm,mxhr->lxhr", selector, bias_table, precision=HIGHEST_PRECISION)
    columns = jnp.arange(WLON, dtype=jnp.int32)
    onehot = (
        columns[None, :, None] - columns[None, None, :] + WLON - 1
        == jnp.arange(2 * WLON - 1, dtype=jnp.int32)[:, None, None]
    ).astype(jnp.float32)
    shifted = lon_rim(lat_rim(paired, half_lat), half_lon)
    windows = window_view(shifted, level_wins, lat_wins, lon_wins, features)
    lat_global = lax.axis_index("lat") * lat_rows + jnp.arange(lat_rows, dtype=jnp.int32)
    lat_flag = (lat_global >= lat_total - half_lat).astype(jnp.int32)
    allowed = group_mask(level_wins, lat_wins, levels, lat_flag)
    bias_win = bias_windows(chosen, onehot, level_wins)
    branch, score_grad = attention_grads(
        windows[0],
        windows[1],
        bias_win,
        allowed,
        norm_gain,
        norm_shift,
        qkv_weight,
        query_bias,
        proj_weight,
    )
    branch, partial_value = (branch, table_terms(score_grad, onehot, selector))
    table_grad = lax.psum(partial_value, "lon")
    lat_count = branch.shape[1]
    lon_count = branch.shape[2]
    field_grad = branch.reshape(level_wins, lat_count, lon_count, WPL, WLAT, WLON, features)
    field_grad = field_grad.transpose(0, 3, 1, 4, 2, 5, 6).reshape(
        levels, lat_count * WLAT, lon_count * WLON, features
    )
    restored = lat_return(lon_return(field_grad, half_lon), half_lat)
    restored = jnp.roll(restored, half_level, axis=0)
    latent_grad = (out_grad.astype(jnp.float32) + restored).astype(jnp.bfloat16)
    return (latent_grad, table_grad)


def solution(mesh):
    in_specs = (
        P(None, "lat", "lon", None),
        P(None, "lat", "lon", None),
        P(),
        P(),
        P(),
        P(),
        P(),
        P("lat", None, None, None),
        P("lat"),
    )
    out_specs = (P(None, "lat", "lon", None), P("lat", None, None, None))
    return jax.shard_map(local, mesh=mesh, in_specs=in_specs, out_specs=out_specs, check_vma=False)
```

profile of v0, /device:TPU:1, one launch (start us, length us, event | category | flops | bytes accessed | tf_op | source)
XLA Modules:
  0.0 864.9 jit_solution(5650325628982896976)
XLA Ops:
  7.2 1.0 fusion.21
  8.2 1.0 fusion.15
  9.2 18.5 %collective-permute-start = (bf16[2,2,3,24,192]{4,3,2,1,0:T(8,128)(2,1)S(1)}, bf16[2,2,3,24,192]{4,3,2,1,0:T(8,128)(2,1)S(1)}, u32[]{:S(2)}, u32[]{:S(2)}) collective-permute-start(bf16[2,2,3,24,192]{4,3,2,1,0:T(8,128)(2,1)S(1)} %get-tuple-element.19), channel_id=1, source_target_pairs={{0,7},{1,0},{2,1},{3,2},{4,3},{5,4},{6,5},{7,6},{8,15},{9,8},{10,9... | collective-permute-start | bytes 331784 | tf_op jit(solution)/shard_map/ppermute | solution.py:18
  29.3 5.0 convolution_bitcast_fusion
  34.3 11.3 %copy.111 = f32[1,1,6,2,6,12,2,6,12]{5,4,3,8,7,6,2,1,0:T(8,128)} copy(f32[1,1,6,2,6,12,2,6,12]{8,7,4,6,3,2,5,0,1:T(8,128)} %convolution_bitcast_fusion) | data formatting | bytes 995328 | tf_op jit(solution)/shard_map/add | solution.py:43
  45.6 5.7 reshape.365
  51.4 2.9 collective-permute-start.1
  54.3 3.0 collective-permute-done.1
  57.9 0.5 multiply_reduce_fusion.2
  60.8 0.4 fusion.42
  61.3 3.3 multiply_reduce_fusion
  64.6 2.7 convolution_convert_fusion
  67.2 0.5 fusion.7
  69.1 0.5 fusion.37
  70.4 2.1 collective-permute-start.2
  72.5 5.0 reshape.366
  77.5 11.0 %copy.102 = f32[6,2,6,12,2,6,12]{6,5,3,4,2,1,0:T(8,128)} copy(f32[6,2,6,12,2,6,12]{3,2,1,6,5,4,0:T(8,128)} %reshape.366) | data formatting | bytes 995328 | tf_op jit(solution)/shard_map/reshape.68
  88.6 1.9 collective-permute-start.3
  90.5 7.2 fusion.1
  97.8 1.0 dot_general.71
  98.9 8.1 collective-permute-done.3
  107.8 0.7 copy.104
  108.5 748.0 %all-reduce.2.cloned.1.call-done = f32[1,1,6,3312]{3,1,2,0:T(1,128)} async-done(((f32[1,1,6,3312]{3,1,2,0:T(1,128)}), f32[1,1,6,3312]{3,1,2,0:T(1,128)}) %all-reduce.2.cloned.1.call-update) | async-done | bytes 79504 | tf_op jit(solution)/shard_map/psum | solution.py:201
  856.5 1.5 copy.136
  (76 shorter events, 6.9 us)
Async XLA Ops:
  7.2 52.7 %copy-start = (bf16[192,576]{1,0:T(8,128)(2,1)S(1)}, bf16[192,576]{1,0:T(8,128)(2,1)}, u32[]{:S(2)}) copy-start(bf16[192,576]{1,0:T(8,128)(2,1)} %param.13) | copy-start | bytes 663556
  7.2 21.2 %copy-start.7 = (f32[1,1,6,3312]{3,1,2,0:T(1,128)S(1)}, f32[1,1,6,3312]{3,1,2,0:T(1,128)}, u32[]{:S(2)}) copy-start(f32[1,1,6,3312]{3,1,2,0:T(1,128)} %param.16) | copy-start | bytes 238468
  7.2 849.3 %all-reduce.2.cloned.1.call-start = ((), (), s32[]{:S(2)}) async-start(), calls=%async_computation | async-start | bytes 159744 | tf_op jit(solution)/shard_map/psum | solution.py:201
  9.2 42.1 %collective-permute-start = (bf16[2,2,3,24,192]{4,3,2,1,0:T(8,128)(2,1)S(1)}, bf16[2,2,3,24,192]{4,3,2,1,0:T(8,128)(2,1)S(1)}, u32[]{:S(2)}, u32[]{:S(2)}) collective-permute-start(bf16[2,2,3,24,192]{4,3,2,1,0:T(8,128)(2,1)S(1)} %get-tuple-element.19), channel_id=1, source_target_pairs={{0,7},{1,0},{2,1},{3,2},{4,3},{5,4},{6,5},{7,6},{8,15},{9,8},{10,9... | collective-permute-start | bytes 331784 | tf_op jit(solution)/shard_map/ppermute | solution.py:18
  51.4 5.9 collective-permute-start.1
  57.4 2.1 copy-start.6
  57.6 2.2 copy-start.8
  57.7 2.2 copy-start.10
  59.3 1.1 copy-start.9
  60.8 3.8 copy-start.3
  64.6 2.7 copy-start.1
  67.2 0.9 copy-start.4
  67.7 1.0 copy-start.5
  70.4 18.1 %collective-permute-start.2 = (bf16[2,6,6,192]{3,0,2,1:T(2,128)(2,1)S(1)}, bf16[2,6,6,192]{3,0,2,1:T(2,128)(2,1)S(1)}, u32[]{:S(2)}, u32[]{:S(2)}) collective-permute-start(bf16[2,6,6,192]{3,0,2,1:T(2,128)(2,1)S(1)} %slice.122), channel_id=1, source_target_pairs={{0,8},{8,16},{16,24},{24,32},{32,40},{40,48},{48,56},{56,64},{64,7... | collective-permute-start | bytes 82952 | tf_op jit(solution)/shard_map/ppermute | solution.py:18
  88.6 18.4 %collective-permute-start.3 = (bf16[2,3,24,192]{3,0,2,1:T(2,128)(2,1)S(1)}, bf16[2,3,24,192]{3,0,2,1:T(2,128)(2,1)S(1)}, u32[]{:S(2)}, u32[]{:S(2)}) collective-permute-start(bf16[2,3,24,192]{3,0,2,1:T(2,128)(2,1)S(1)} %fusion.27), channel_id=1, source_target_pairs={{0,1},{1,2},{2,3},{3,4},{4,5},{5,6},{6,7},{7,0},{8,9},{9,10},{10,1... | collective-permute-start | bytes 165896 | tf_op jit(solution)/shard_map/ppermute | solution.py:18
  97.7 9.7 %copy-start.2 = (bf16[2,6,24,192]{3,2,1,0:T(8,128)(2,1)S(1)}, bf16[2,6,24,192]{3,2,1,0:T(8,128)(2,1)}, u32[]{:S(2)}) copy-start(bf16[2,6,24,192]{3,2,1,0:T(8,128)(2,1)} %param.10) | copy-start | bytes 331780
Sparse Core Ops, SparseCore 0:
  99.0 757.4 all-reduce.1
where the time goes:
time: 867 us; the launch traced here: 865 us
  waiting for transfers between devices  759 us (88%)
  local copies, waits for them, and re-layouts  39.9 us (5%)
  starting transfers between devices  25.4 us (3%)
  matrix products  20.4 us (2%)
  between operations  15.2 us (2%)
    psum x1, waiting for transfers between devices, local(): table_grad = lax.psum(partial_value, 'lon')  748 us
    ppermute x4, starting transfers between devices, from_behind(): lax.ppermute(array, axis, [(i, (i + by) % size) for i in range(size)])  25.3 us
  transfers between devices with their start and end apart: 5, of which 3 were waited for; matrix products, arithmetic and copies ran while one was open for 6% of the time, Pallas kernels for 0%

commit v1 on v0

v1 whole, which is shorter than its diff:
```python
import functools

import jax
import jax.numpy as jnp
import ml_dtypes
import numpy as np
from jax import lax
from jax.experimental import pallas as pl
from jax.experimental.pallas import tpu as pltpu
from jax.sharding import PartitionSpec as P

HEADS = 6
D = 192
WLAT = 6
WLON = 12
ROWS = 6
COLS = 24
REL = 3312
SPAN = 2 * WLON - 1
FLAT = SPAN * WLAT * WLAT
EPSILON = 1e-05
SCALE = 32 ** (-0.5)
TOK = ROWS * COLS
WTOK = 96
BOTH = 2 * WTOK
FWD = ((0, 176), (176, 64), (240, 64))
FWD_ROWS = 304
RET = ((0, 96), (96, 32), (128, 32))
RET_ROWS = 160
LANES = HEADS * 128
WIDE = 896
MASKED = -1e30
MESH = pl.DeviceIdType.MESH


def constants():
    def token(row, col):
        return row * COLS + col

    def wrow(rolled_row, rolled_col):
        return (rolled_col // WLON) * WTOK + (rolled_col % WLON) * 8 + rolled_row

    lat = [(r, c) for r in range(3) for c in range(6, COLS)]
    diag = [(r, c) for r in range(3) for c in range(6)]
    lon = [(r, c) for r in range(3, ROWS) for c in range(6)]
    groups = (
        [(token(r, c), wrow(r + 3, c - 6)) for r, c in lat],
        [(token(r, c), wrow(r + 3, c + 18)) for r, c in diag],
        [(token(r, c), wrow(r - 3, c + 18)) for r, c in lon],
    )
    own = [(token(r, c), wrow(r - 3, c - 6)) for r in range(3, ROWS) for c in range(6, COLS)]

    pack = np.zeros((FWD_ROWS, 3 * TOK), np.float32)
    take_remote = np.zeros((3 * BOTH, FWD_ROWS), np.float32)
    ret_pack = np.zeros((RET_ROWS, 3 * BOTH), np.float32)
    put_remote = np.zeros((3 * TOK, RET_ROWS), np.float32)
    for (at, _), (back, _), group in zip(FWD, RET, groups):
        n = len(group)
        for k, (t, w) in enumerate(group):
            for part in range(3):
                pack[at + part * n + k, part * TOK + t] = 1
                take_remote[part * BOTH + w, at + part * n + k] = 1
            ret_pack[back + k, w] = 1
            put_remote[t, back + k] = 1
            high = k >= n // 2
            slot = back + n + k % (n // 2)
            ret_pack[slot, (2 if high else 1) * BOTH + w] = 1
            put_remote[(2 if high else 1) * TOK + t, slot] = 1
    take_own = np.zeros((3 * BOTH, 3 * TOK), np.float32)
    put_own = np.zeros((TOK, BOTH), np.float32)
    for t, w in own:
        put_own[t, w] = 1
        for part in range(3):
            take_own[part * BOTH + w, part * TOK + t] = 1
    tails = np.zeros((2, D, 128), np.float32)
    for i in range(64):
        tails[0, 128 + i, i] = 1
        tails[1, 128 + i, 64 + i] = 1
    spread = np.zeros((256, WIDE), np.float32)
    for d in range(SPAN):
        for a in range(WLAT):
            spread[8 * d + a, SPAN * WLAT * a + d] = 1
    qkv_pad = np.zeros((3 * D, LANES), np.float32)
    for part in range(3):
        for i in range(D):
            qkv_pad[part * D + i, part * 256 + i] = 1
    proj_pad = np.zeros((D, 256), np.float32)
    for i in range(D):
        proj_pad[i, i if i < 128 else 64 + i] = 1
    head_mask = np.zeros((16, 256), np.float32)
    for h in range(HEADS):
        head_mask[h, h * 32 : (h + 1) * 32] = 1
    matrices = (
        pack,
        tails.reshape(2 * D, 128),
        take_own,
        take_remote,
        ret_pack,
        put_own,
        put_remote,
        spread,
        qkv_pad,
        proj_pad,
        head_mask,
    )
    return tuple(m.astype(ml_dtypes.bfloat16) for m in matrices)


def dot(a, b):
    return jnp.dot(a, b, preferred_element_type=jnp.float32)


def dot_nt(a, b):
    return lax.dot_general(a, b, (((1,), (1,)), ((), ())), preferred_element_type=jnp.float32)


def dot_tn(a, b):
    return lax.dot_general(a, b, (((0,), (0,)), ((), ())), preferred_element_type=jnp.float32)


def low(a):
    return a.astype(jnp.bfloat16)


def kernel(n_lon, n_lat, n_in, *refs):
    ins, refs = refs[:n_in], refs[n_in:]
    (grad_out, table_out), refs = refs[:2], refs[2:]
    held, refs = refs[:n_in], refs[n_in:]
    (
        send_buf,
        recv_buf,
        ret_send,
        ret_recv,
        x_own,
        bias,
        table_pad,
        fold_buf,
        vecs,
        w_qkv,
        w_proj,
        q_heads,
        u_heads,
        branch_buf,
        red_src,
        red_in,
        z_slots,
        all_slots,
        in_sem,
        fwd_send,
        fwd_recv,
        back_send,
        back_recv,
        red_send,
        red_recv,
        z_send,
        z_recv,
        all_send,
        all_recv,
    ) = refs
    (
        latent,
        out_grad,
        gain,
        shift,
        qkv_weight,
        query_bias,
        proj_weight,
        bias_table,
        pack,
        tails,
        take_own,
        take_remote,
        ret_pack,
        put_own,
        put_remote,
        spread,
        qkv_pad,
        proj_pad,
        head_mask,
    ) = held

    lon, lat = lax.axis_index("lon"), lax.axis_index("lat")
    lon_m, lon_p = lax.rem(lon + n_lon - 1, n_lon), lax.rem(lon + 1, n_lon)
    lat_m, lat_p = lax.rem(lat + n_lat - 1, n_lat), lax.rem(lat + 1, n_lat)

    def at(lon_at, lat_at):
        return {"lon": lon_at, "lat": lat_at}

    before = (at(lon, lat_m), at(lon_m, lat_m), at(lon_m, lat))
    behind = (at(lon, lat_p), at(lon_p, lat_p), at(lon_p, lat))
    z_me = lax.rem(lon // 2, 8)
    y_me = lon // 16
    plane_me = y_me * 2 + lax.rem(lon, 2)

    def plane_peer(step):
        rank = lax.rem(plane_me + step, 8)
        return rank, at(((rank // 2) * 8 + z_me) * 2 + lax.rem(rank, 2), lat)

    def z_peer(step):
        z = lax.rem(z_me + step, 8)
        return at((y_me * 8 + z) * 2 + lax.rem(lon, 2), lat)

    barrier = pltpu.get_barrier_semaphore()
    everyone = list(before) + list(behind)
    everyone += [z_peer(s) for s in range(1, 8)] + [plane_peer(s)[1] for s in range(1, 8)]
    for peer in everyone:
        pl.semaphore_signal(barrier, inc=1, device_id=peer, device_id_type=MESH)

    loads = [pltpu.make_async_copy(s, d, in_sem.at[i]) for i, (s, d) in enumerate(zip(ins, held))]
    order = [0, 1, 9, 8, 10, 4, 16, 6, 17, 15, 7, 2, 3, 5, 18, 11, 12, 13, 14]
    for i in order:
        loads[i].start()
    for i in (0, 1, 9, 8):
        loads[i].wait()

    sources = []
    for p in range(2):
        rows = pl.ds((1 - p) * TOK, TOK)
        mixed = dot(latent[rows, :], tails[0:D, :]) + dot(out_grad[rows, :], tails[D : 2 * D, :])
        source = jnp.concatenate([latent[rows, 0:128], out_grad[rows, 0:128], low(mixed)], 0)
        sources.append(source)
        send_buf[p] = low(dot(pack[...], source))

    pl.semaphore_wait(barrier, len(everyone))
    forward = []
    for p in range(2):
        for g, (start, size) in enumerate(FWD):
            copy = pltpu.make_async_remote_copy(
                src_ref=send_buf.at[p, pl.ds(start, size)],
                dst_ref=recv_buf.at[p, pl.ds(start, size)],
                send_sem=fwd_send.at[p, g],
                recv_sem=fwd_recv.at[p, g],
                device_id=before[g],
                device_id_type=MESH,
            )
            copy.start()
            forward.append(copy)

    for i in order:
        if i not in (0, 1, 9, 8):
            loads[i].wait()

    for p in range(2):
        x_own[p] = dot(take_own[...], sources[p])

    w_qkv[0:D, :] = low(dot(qkv_weight[...], qkv_pad[...]))
    w_qkv[D:256, :] = jnp.zeros((256 - D, LANES), jnp.bfloat16)
    w_proj[0:D, :] = low(dot(proj_weight[...], proj_pad[...]))
    w_proj[D:256, :] = jnp.zeros((256 - D, 256), jnp.bfloat16)
    vecs[...] = jnp.zeros((8, 256), jnp.float32)
    vecs[0:1, 0:D] = gain[...]
    vecs[1:2, 0:D] = shift[...]
    vecs[2:3, 0:D] = query_bias[...]
    q_heads[...] = jnp.zeros((LANES, 256), jnp.bfloat16)
    u_heads[...] = jnp.zeros((LANES, 256), jnp.bfloat16)

    lane8 = lax.broadcasted_iota(jnp.int32, (8, 128), 1)
    row8 = lax.broadcasted_iota(jnp.int32, (8, 128), 0)
    last = (lat == n_lat - 1).astype(jnp.int32)
    query_half = (lax.rem(lane8, 8) >= 3).astype(jnp.int32)
    key_half = (row8 >= 3).astype(jnp.int32)
    left_out = (row8 >= WLAT).astype(jnp.int32) + last * (query_half ^ key_half) > 0

    for p in range(2):
        table_pad[...] = jnp.zeros((8, WIDE), jnp.float32)
        if p == 0:
            table_pad[0:HEADS, :] = bias_table[:, 0:WIDE]
        else:
            table_pad[0:HEADS, 0 : REL - 2432] = bias_table[:, 2432:REL]
        entries = table_pad[...]
        for b in range(8):
            if b < WLAT:
                moved = pltpu.roll(entries, (2 * WIDE - SPAN * b - 52 * p) % WIDE, 1)
                top = low(moved)
                rest = low(moved - top.astype(jnp.float32))
                row = dot_nt(top, spread[...]) + dot_nt(rest, spread[...])
            else:
                row = jnp.zeros((8, 256), jnp.float32)
            fold_buf[0, 8 * b : 8 * b + 8, :] = row[:, 0:128]
            fold_buf[1, 8 * b : 8 * b + 8, :] = row[:, 128:256]
        for h in range(HEADS):
            near = fold_buf[0, pl.ds(h, 8, stride=8), :]
            far = fold_buf[1, pl.ds(h, 8, stride=8), :]
            for r in range(WLON):
                s = 8 * (WLON - 1 - r)
                if s:
                    block = pltpu.roll(jnp.where(lane8 >= s, near, far), 128 - s, 1)
                else:
                    block = near
                bias[p, 8 * r : 8 * r + 8, 128 * h : 128 * h + 128] = jnp.where(left_out, MASKED, block)

    gain_w, shift_w, query_w = vecs[0:1, :], vecs[1:2, :], vecs[2:3, :]
    below64 = lax.broadcasted_iota(jnp.int32, (BOTH, 128), 1) < 64
    low_lane = lax.broadcasted_iota(jnp.int32, (BOTH, 256), 1) < D
    backward = []
    flats = []
    own_parts = []

    for p in range(2):
        for g in range(3):
            forward[3 * p + g].wait_recv()
        tokens = x_own[p] + dot(take_remote[...], recv_buf[p])
        x_a, x_b, x_c = tokens[0:BOTH], tokens[BOTH : 2 * BOTH], tokens[2 * BOTH :]
        tail = jnp.where(below64, x_c, 0.0)
        center = (jnp.sum(x_a, 1, keepdims=True) + jnp.sum(tail, 1, keepdims=True)) * (1.0 / D)
        c_a = x_a - center
        c_t = jnp.where(below64, x_c - center, 0.0)
        spread_sq = (
            jnp.sum(c_a * c_a, 1, keepdims=True) + jnp.sum(c_t * c_t, 1, keepdims=True)
        ) * (1.0 / D)
        inverse = lax.rsqrt(spread_sq + EPSILON)
        normed = jnp.concatenate([c_a, c_t], 1) * inverse
        hidden = low(normed * gain_w + shift_w)
        projected = dot(hidden, w_qkv[...])
        queries = low(projected[:, 0:256] + query_w)
        keys = low(projected[:, 256:512])
        values = low(projected[:, 512:768])
        incoming = low(jnp.concatenate([x_b, x_c], 1))
        upstream = low(dot_nt(incoming, w_proj[...]))

        score_lows, prob_lows = [], []
        score_sum = None
        for w in range(2):
            span = slice(w * WTOK, (w + 1) * WTOK)
            for h in range(HEADS):
                mask = head_mask[h : h + 1, :]
                q_heads[pl.ds(h * 128, WTOK), :] = queries[span] * mask
                u_heads[pl.ds(h * 128, WTOK), :] = upstream[span] * mask
            scores = dot_nt(keys[span], q_heads[...]) * SCALE + bias[p]
            weights = jnp.exp(scores)
            probs = weights * (1.0 / jnp.sum(weights, 0, keepdims=True))
            prob_grad = dot_nt(values[span], u_heads[...])
            inner = jnp.sum(probs * prob_grad, 0, keepdims=True)
            score_grad = probs * (prob_grad - inner)
            score_sum = score_grad if score_sum is None else score_sum + score_grad
            score_low = low(score_grad)
            value_g = dot(low(probs), u_heads[...])
            key_g = dot(score_low, q_heads[...]) * SCALE
            query_all = dot_tn(score_low, keys[span])
            query_g = None
            for h in range(HEADS):
                term = query_all[h * 128 : h * 128 + WTOK] * head_mask[h : h + 1, :].astype(jnp.float32)
                query_g = term if query_g is None else query_g + term
            score_lows.append(jnp.concatenate([low(query_g * SCALE), low(key_g), low(value_g)], 1))

        for h in range(HEADS):
            near = far = None
            for r in range(WLON):
                s = 8 * (WLON - 1 - r)
                block = score_sum[8 * r : 8 * r + 8, 128 * h : 128 * h + 128]
                if s:
                    block = pltpu.roll(block, s, 1)
                    wrapped = jnp.where(lane8 < s, block, 0.0)
                    block = jnp.where(lane8 < s, 0.0, block)
                    far = wrapped if far is None else far + wrapped
                near = block if near is None else near + block
            fold_buf[0, 8 * h : 8 * h + 8, :] = near
            fold_buf[1, 8 * h : 8 * h + 8, :] = far
        by_row = [
            jnp.concatenate([fold_buf[part, pl.ds(b, 8, stride=8), :] for part in range(2)], 1)
            for b in range(WLAT)
        ]
        lines = dot(low(jnp.concatenate(by_row, 0)), spread[...])
        flat = None
        for b in range(WLAT):
            line = lines[8 * b : 8 * b + 8]
            if b or p:
                line = pltpu.roll(line, SPAN * b + 52 * p, 1)
            flat = line if flat is None else flat + line
        flats.append(flat)

        if p == 1:
            for c in range(8):
                for half in range(2):
                    tile = 2 * c + half
                    if tile < 14:
                        part = flats[tile // 7][:, 128 * (tile % 7) : 128 * (tile % 7) + 128]
                    else:
                        part = jnp.zeros((8, 128), jnp.float32)
                    all_slots[c, 8 * half : 8 * half + 8, :] = part
                red_src[c] = low(all_slots[c])
            reduced = []
            for s in range(1, 8):
                rank, peer = plane_peer(s)
                copy = pltpu.make_async_remote_copy(
                    src_ref=red_src.at[rank],
                    dst_ref=red_in.at[s - 1],
                    send_sem=red_send.at[s - 1],
                    recv_sem=red_recv.at[s - 1],
                    device_id=peer,
                    device_id_type=MESH,
                )
                copy.start()
                reduced.append(copy)

        hidden_grad = dot_nt(jnp.concatenate(score_lows, 0), w_qkv[...])
        scaled = hidden_grad * gain_w
        mean_g = jnp.sum(scaled, 1, keepdims=True) * (1.0 / D)
        mean_gn = jnp.sum(scaled * normed, 1, keepdims=True) * (1.0 / D)
        branch = jnp.where(low_lane, inverse * (scaled - mean_g - normed * mean_gn), 0.0)
        second = branch[:, 128:256]
        stacked = jnp.concatenate([branch[:, 0:128], second, pltpu.roll(second, 64, 1)], 0)
        ret_send[p] = low(dot(ret_pack[...], low(stacked)))
        for g, (start, size) in enumerate(RET):
            copy = pltpu.make_async_remote_copy(
                src_ref=ret_send.at[p, pl.ds(start, size)],
                dst_ref=ret_recv.at[p, pl.ds(start, size)],
                send_sem=back_send.at[p, g],
                recv_sem=back_recv.at[p, g],
                device_id=behind[g],
                device_id_type=MESH,
            )
            copy.start()
            backward.append(copy)
        branch_buf[p] = low(branch)

    for copy in reduced:
        copy.wait_recv()
    total = red_src[plane_me].astype(jnp.float32)
    for s in range(7):
        total = total + red_in[s].astype(jnp.float32)
    z_slots[z_me] = low(total)
    along = []
    for s in range(1, 8):
        copy = pltpu.make_async_remote_copy(
            src_ref=z_slots.at[z_me],
            dst_ref=z_slots.at[z_me],
            send_sem=z_send.at[s - 1],
            recv_sem=z_recv.at[s - 1],
            device_id=z_peer(s),
            device_id_type=MESH,
        )
        copy.start()
        along.append(copy)

    for p in range(2):
        rows = pl.ds((1 - p) * TOK, TOK)
        own = dot(put_own[...], branch_buf[p])
        own_parts.append(
            (
                own[:, 0:128] + out_grad[rows, 0:128].astype(jnp.float32),
                own[:, 128:D] + out_grad[rows, 128:D].astype(jnp.float32),
            )
        )

    for copy in along:
        copy.wait_recv()
    total = z_slots[0].astype(jnp.float32)
    for z in range(1, 8):
        total = total + z_slots[z].astype(jnp.float32)
    all_slots[plane_me] = total
    gathered = []
    for s in range(1, 8):
        _, peer = plane_peer(s)
        copy = pltpu.make_async_remote_copy(
            src_ref=all_slots.at[plane_me],
            dst_ref=all_slots.at[plane_me],
            send_sem=all_send.at[s - 1],
            recv_sem=all_recv.at[s - 1],
            device_id=peer,
            device_id_type=MESH,
        )
        copy.start()
        gathered.append(copy)

    for p in range(2):
        rows = pl.ds((1 - p) * TOK, TOK)
        for g in range(3):
            backward[3 * p + g].wait_recv()
        got = dot(put_remote[...], ret_recv[p])
        first, second = own_parts[p]
        grad_out[rows, 0:128] = low(first + got[0:TOK])
        rest = got[TOK : 2 * TOK] + pltpu.roll(got[2 * TOK :], 64, 1)
        grad_out[rows, 128:D] = low(second + rest[:, 0 : D - 128])

    table_out[...] = jnp.zeros((HEADS, REL), jnp.float32)
    for copy in gathered:
        copy.wait_recv()
    for tile in range(14):
        entries = all_slots[tile // 2, pl.ds(8 * (tile % 2), HEADS), :]
        start = 128 * tile if tile < 7 else 2432 + 128 * (tile - 7)
        size = min(128, REL - start)
        table_out[:, start : start + size] = entries[:, 0:size]

    for copy in forward + backward + reduced + along + gathered:
        copy.wait_send()


def local(n_lon, n_lat, latent, out_grad, gain, shift, qkv_weight, query_bias, proj_weight, bias_table, band_rows):
    del band_rows
    consts = [jnp.asarray(c) for c in constants()]
    args = [
        latent.reshape(2 * TOK, D),
        out_grad.reshape(2 * TOK, D),
        gain.reshape(1, D),
        shift.reshape(1, D),
        qkv_weight,
        query_bias.reshape(1, D),
        proj_weight,
        bias_table.reshape(HEADS, REL),
    ] + consts
    bf16, f32 = jnp.bfloat16, jnp.float32
    dma = pltpu.SemaphoreType.DMA
    scratch = [pltpu.VMEM(a.shape, a.dtype) for a in args] + [
        pltpu.VMEM((2, FWD_ROWS, 128), bf16),
        pltpu.VMEM((2, FWD_ROWS, 128), bf16),
        pltpu.VMEM((2, RET_ROWS, 128), bf16),
        pltpu.VMEM((2, RET_ROWS, 128), bf16),
        pltpu.VMEM((2, 3 * BOTH, 128), f32),
        pltpu.VMEM((2, WTOK, LANES), f32),
        pltpu.VMEM((8, WIDE), f32),
        pltpu.VMEM((2, 64, 128), f32),
        pltpu.VMEM((8, 256), f32),
        pltpu.VMEM((256, LANES), bf16),
        pltpu.VMEM((256, 256), bf16),
        pltpu.VMEM((LANES, 256), bf16),
        pltpu.VMEM((LANES, 256), bf16),
        pltpu.VMEM((2, BOTH, 256), bf16),
        pltpu.VMEM((8, 16, 128), bf16),
        pltpu.VMEM((7, 16, 128), bf16),
        pltpu.VMEM((8, 16, 128), bf16),
        pltpu.VMEM((8, 16, 128), f32),
        dma((len(args),)),
        dma((2, 3)),
        dma((2, 3)),
        dma((2, 3)),
        dma((2, 3)),
        dma((7,)),
        dma((7,)),
        dma((7,)),
        dma((7,)),
        dma((7,)),
        dma((7,)),
    ]
    grad, table = pl.pallas_call(
        functools.partial(kernel, n_lon, n_lat, len(args)),
        out_shape=(
            jax.ShapeDtypeStruct((2 * TOK, D), bf16),
            jax.ShapeDtypeStruct((HEADS, REL), f32),
        ),
        in_specs=[pl.BlockSpec(memory_space=pl.ANY)] * len(args),
        out_specs=(pl.BlockSpec(memory_space=pltpu.VMEM), pl.BlockSpec(memory_space=pltpu.VMEM)),
        scratch_shapes=scratch,
        compiler_params=pltpu.CompilerParams(
            collective_id=0, has_side_effects=True, vmem_limit_bytes=50 * 1024 * 1024
        ),
    )(*args)
    return grad.reshape(latent.shape), table.reshape(bias_table.shape)


def solution(mesh):
    in_specs = (
        P(None, "lat", "lon", None),
        P(None, "lat", "lon", None),
        P(),
        P(),
        P(),
        P(),
        P(),
        P("lat", None, None, None),
        P("lat"),
    )
    out_specs = (P(None, "lat", "lon", None), P("lat", None, None, None))
    body = functools.partial(local, mesh.shape["lon"], mesh.shape["lat"])
    return jax.shard_map(body, mesh=mesh, in_specs=in_specs, out_specs=out_specs, check_vma=False)
```

time: 867 us -> 66.3 us (0.08)
  waiting for transfers between devices: 759 us -> 0 us
  Pallas kernels: 0 us -> 49.3 us
  starting transfers between devices: 25.4 us -> 0 us
  local copies, waits for them, and re-layouts: 39.9 us -> 15.7 us
  matrix products: 20.4 us -> 0 us
  between operations: 15.2 us -> 0.69 us
    psum x1 -> x0, waiting for transfers between devices: 748 us -> none  [local(): table_grad = lax.psum(partial_value, 'lon')]
    pallas_call x0 -> x1, Pallas kernels: none -> 49.3 us  [local(): pl.pallas_call(functools.partial(kernel, n_lon, n_lat, len(args)), out_sh...]
    ppermute x4 -> x0, starting transfers between devices: 25.3 us -> none  [from_behind(): lax.ppermute(array, axis, [(i, (i + by) % size) for i in range(size)])]
    dot_general x9 -> x0, matrix products: 17.1 us -> none  [the longest x1 7.2 us: table_terms(): jnp.einsum('xlhpaoqbr,dor->xlhpqabd', unfolded, onehot, precision=HIGHEST...]
    add x2 -> x0, local copies, waits for them, and re-layouts: 17 us -> none  [attention_grads(): factor * jnp.einsum('...ihe,...jhe->...hij', queries, keys_low, preferred...]
    another operation x2 -> x0, local copies, waits for them, and re-layouts: 16 us -> none
    unnamed x24 -> x37, local copies, waits for them, and re-layouts: 2.57 us -> 15.7 us
    ppermute x4 -> x0, waiting for transfers between devices: 11.1 us -> none  [from_behind(): lax.ppermute(array, axis, [(i, (i + by) % size) for i in range(size)])]
  transfers between devices with their start and end apart: 5 -> 0, of which waited for: 3 -> 0; matrix products, arithmetic and copies ran while one was open for 6% -> 0% of each run, Pallas kernels for 0% -> 0%
where the time goes in v1:
time: 66.3 us; the launch traced here: 65.7 us
  Pallas kernels  49.3 us (74%)
  local copies, waits for them, and re-layouts  15.7 us (24%)
  between operations  0.69 us (1%)
    pallas_call x1, Pallas kernels, local(): pl.pallas_call(functools.partial(kernel, n_lon, n_lat, len(args)), out_sh...  49.3 us
    unnamed x37, local copies, waits for them, and re-layouts  15.7 us

profile of v1, /device:TPU:1, one launch (start us, length us, event | category | flops | bytes accessed | tf_op | source)
XLA Modules:
  0.0 65.7 jit_solution(7641642621953106764)
XLA Ops:
  0.6 0.0 copy-start.13
  0.6 0.0 copy-start.6
  0.7 0.9 %copy.24 = f32[1,1,6,3312]{3,2,1,0:T(8,128)S(1)} copy(f32[1,1,6,3312]{3,1,2,0:T(1,128)} %param.27) | data formatting | bytes 158976
  1.6 0.0 copy-done.13
  1.6 0.0 copy-done.6
  1.6 0.0 copy-start
  1.6 1.1 %copy-done = bf16[576,432]{1,0:T(8,128)(2,1)S(1)} copy-done((bf16[576,432]{1,0:T(8,128)(2,1)S(1)}, bf16[576,432]{1,0:T(8,128)(2,1)}, u32[]{:S(2)}) %copy-start) | copy-done | bytes 497688
  2.7 1.0 %copy-done.1 = bf16[256,896]{1,0:T(8,128)(2,1)S(1)} copy-done((bf16[256,896]{1,0:T(8,128)(2,1)S(1)}, bf16[256,896]{1,0:T(8,128)(2,1)}, u32[]{:S(2)}) %copy-start.1) | copy-done | bytes 458776
  3.7 1.0 %copy-done.2 = bf16[576,304]{1,0:T(8,128)(2,1)S(1)} copy-done((bf16[576,304]{1,0:T(8,128)(2,1)S(1)}, bf16[576,304]{1,0:T(8,128)(2,1)}, u32[]{:S(2)}) %copy-start.2) | copy-done | bytes 350232
  4.7 1.0 %copy-done.3 = bf16[304,432]{1,0:T(8,128)(2,1)S(1)} copy-done((bf16[304,432]{1,0:T(8,128)(2,1)S(1)}, bf16[304,432]{1,0:T(8,128)(2,1)}, u32[]{:S(2)}) %copy-start.3) | copy-done | bytes 262680
  5.7 0.9 %copy-done.4 = bf16[192,576]{1,0:T(8,128)(2,1)S(1)} copy-done((bf16[192,576]{1,0:T(8,128)(2,1)S(1)}, bf16[192,576]{1,0:T(8,128)(2,1)}, u32[]{:S(2)}) %copy-start.4) | copy-done | bytes 221208
  6.6 0.9 %copy-done.5 = bf16[432,160]{1,0:T(8,128)(2,1)S(1)} copy-done((bf16[432,160]{1,0:T(8,128)(2,1)S(1)}, bf16[432,160]{1,0:T(8,128)(2,1)}, u32[]{:S(2)}) %copy-start.5) | copy-done | bytes 138264
  7.6 0.9 %copy-done.7 = bf16[2,6,24,192]{3,2,1,0:T(8,128)(2,1)S(1)} copy-done((bf16[2,6,24,192]{3,2,1,0:T(8,128)(2,1)S(1)}, bf16[2,6,24,192]{3,2,1,0:T(8,128)(2,1)}, u32[]{:S(2)}) %copy-start.7) | copy-done | bytes 110616
  8.5 0.9 %copy-done.8 = bf16[2,6,24,192]{3,2,1,0:T(8,128)(2,1)S(1)} copy-done((bf16[2,6,24,192]{3,2,1,0:T(8,128)(2,1)S(1)}, bf16[2,6,24,192]{3,2,1,0:T(8,128)(2,1)}, u32[]{:S(2)}) %copy-start.8) | copy-done | bytes 110616
  9.4 0.9 %copy-done.9 = bf16[192,192]{1,0:T(8,128)(2,1)S(1)} copy-done((bf16[192,192]{1,0:T(8,128)(2,1)S(1)}, bf16[192,192]{1,0:T(8,128)(2,1)}, u32[]{:S(2)}) %copy-start.9) | copy-done | bytes 73752
  10.3 0.9 %copy-done.10 = bf16[192,256]{1,0:T(8,128)(2,1)S(1)} copy-done((bf16[192,256]{1,0:T(8,128)(2,1)S(1)}, bf16[192,256]{1,0:T(8,128)(2,1)}, u32[]{:S(2)}) %copy-start.10) | copy-done | bytes 98328
  11.2 0.9 %copy-done.11 = bf16[384,128]{1,0:T(8,128)(2,1)S(1)} copy-done((bf16[384,128]{1,0:T(8,128)(2,1)S(1)}, bf16[384,128]{1,0:T(8,128)(2,1)}, u32[]{:S(2)}) %copy-start.11) | copy-done | bytes 98328
  12.1 0.9 %copy-done.12 = bf16[144,192]{1,0:T(8,128)(2,1)S(1)} copy-done((bf16[144,192]{1,0:T(8,128)(2,1)S(1)}, bf16[144,192]{1,0:T(8,128)(2,1)}, u32[]{:S(2)}) %copy-start.12) | copy-done | bytes 55320
  13.0 0.7 %copy-done.14 = f32[192]{0:T(256)S(1)} copy-done((f32[192]{0:T(256)S(1)}, f32[192]{0:T(256)}, u32[]{:S(2)}) %copy-start.14) | copy-done | bytes 792
  13.6 0.7 %copy-done.15 = f32[192]{0:T(256)S(1)} copy-done((f32[192]{0:T(256)S(1)}, f32[192]{0:T(256)}, u32[]{:S(2)}) %copy-start.15) | copy-done | bytes 792
  14.3 0.7 %copy-done.16 = f32[192]{0:T(256)S(1)} copy-done((f32[192]{0:T(256)S(1)}, f32[192]{0:T(256)}, u32[]{:S(2)}) %copy-start.16) | copy-done | bytes 792
  15.0 49.3 %shard_map.194 = (bf16[288,192]{1,0:T(8,128)(2,1)S(1)}, f32[6,3312]{1,0:T(8,128)S(1)}) custom-call(bf16[288,192]{1,0:T(8,128)(2,1)S(1)} %bitcast.11, bf16[288,192]{1,0:T(8,128)(2,1)S(1)} %bitcast.12, f32[1,192]{1,0:T(1,128)S(1)} %bitcast.15, f32[1,192]{1,0:T(1,128)S(1)} %bitcast.16, bf16[192,576]{1,0:T(8,128)(2,1)S(1)} %copy-done.4, f32[1,192]{1,0:T(1,128)S(1)} %bitcast.17, ...), custom_call_target="tpu_custom_call" | custom-call | tf_op jit(solution)/shard_map/pallas_call | solution.py:535
  64.3 0.7 %copy.21 = f32[1,1,6,3312]{3,1,2,0:T(1,128)} copy(f32[1,1,6,3312]{3,2,1,0:T(8,128)S(1)} %bitcast.14) | data formatting | bytes 158976
  65.1 0.7 %copy.26 = bf16[2,6,24,192]{3,2,1,0:T(8,128)(2,1)} copy(bf16[2,6,24,192]{3,2,1,0:T(8,128)(2,1)S(1)} %bitcast.13) | data formatting | bytes 221184
  (14 shorter events, 0.0 us)
Async XLA Ops:
  0.6 1.0 %copy-start.13 = (bf16[16,256]{1,0:T(8,128)(2,1)S(1)}, bf16[16,256]{1,0:T(8,128)(2,1)}, u32[]{:S(2)}) copy-start(bf16[16,256]{1,0:T(8,128)(2,1)} %constant.32.clone.refs_18_) | copy-start | bytes 24580
  0.6 1.0 %copy-start.6 = (bf16[160,576]{1,0:T(8,128)(2,1)S(1)}, bf16[160,576]{1,0:T(8,128)(2,1)}, u32[]{:S(2)}) copy-start(bf16[160,576]{1,0:T(8,128)(2,1)} %constant.26.clone.refs_12_) | copy-start | bytes 552964
  1.6 1.1 %copy-start = (bf16[576,432]{1,0:T(8,128)(2,1)S(1)}, bf16[576,432]{1,0:T(8,128)(2,1)}, u32[]{:S(2)}) copy-start(bf16[576,432]{1,0:T(8,128)(2,1)} %constant.24.clone.refs_10_) | copy-start | bytes 1492996
  2.7 1.0 %copy-start.1 = (bf16[256,896]{1,0:T(8,128)(2,1)S(1)}, bf16[256,896]{1,0:T(8,128)(2,1)}, u32[]{:S(2)}) copy-start(bf16[256,896]{1,0:T(8,128)(2,1)} %constant.29.clone.refs_15_) | copy-start | bytes 1376260
  3.7 1.0 %copy-start.2 = (bf16[576,304]{1,0:T(8,128)(2,1)S(1)}, bf16[576,304]{1,0:T(8,128)(2,1)}, u32[]{:S(2)}) copy-start(bf16[576,304]{1,0:T(8,128)(2,1)} %constant.25.clone.refs_11_) | copy-start | bytes 1050628
  4.7 1.0 %copy-start.3 = (bf16[304,432]{1,0:T(8,128)(2,1)S(1)}, bf16[304,432]{1,0:T(8,128)(2,1)}, u32[]{:S(2)}) copy-start(bf16[304,432]{1,0:T(8,128)(2,1)} %constant.22.clone.refs_8_) | copy-start | bytes 787972
  5.7 0.9 %copy-start.4 = (bf16[192,576]{1,0:T(8,128)(2,1)S(1)}, bf16[192,576]{1,0:T(8,128)(2,1)}, u32[]{:S(2)}) copy-start(bf16[192,576]{1,0:T(8,128)(2,1)} %refs_4_.1) | copy-start | bytes 663556
  6.6 0.9 %copy-start.5 = (bf16[432,160]{1,0:T(8,128)(2,1)S(1)}, bf16[432,160]{1,0:T(8,128)(2,1)}, u32[]{:S(2)}) copy-start(bf16[432,160]{1,0:T(8,128)(2,1)} %constant.28.clone.refs_14_) | copy-start | bytes 414724
  7.6 0.9 %copy-start.7 = (bf16[2,6,24,192]{3,2,1,0:T(8,128)(2,1)S(1)}, bf16[2,6,24,192]{3,2,1,0:T(8,128)(2,1)}, u32[]{:S(2)}) copy-start(bf16[2,6,24,192]{3,2,1,0:T(8,128)(2,1)} %param.20) | copy-start | bytes 331780
  8.5 0.9 %copy-start.8 = (bf16[2,6,24,192]{3,2,1,0:T(8,128)(2,1)S(1)}, bf16[2,6,24,192]{3,2,1,0:T(8,128)(2,1)}, u32[]{:S(2)}) copy-start(bf16[2,6,24,192]{3,2,1,0:T(8,128)(2,1)} %param.21) | copy-start | bytes 331780
  9.4 0.9 %copy-start.9 = (bf16[192,192]{1,0:T(8,128)(2,1)S(1)}, bf16[192,192]{1,0:T(8,128)(2,1)}, u32[]{:S(2)}) copy-start(bf16[192,192]{1,0:T(8,128)(2,1)} %refs_6_.1) | copy-start | bytes 221188
  10.3 0.9 %copy-start.10 = (bf16[192,256]{1,0:T(8,128)(2,1)S(1)}, bf16[192,256]{1,0:T(8,128)(2,1)}, u32[]{:S(2)}) copy-start(bf16[192,256]{1,0:T(8,128)(2,1)} %constant.31.clone.refs_17_) | copy-start | bytes 294916
  11.2 0.9 %copy-start.11 = (bf16[384,128]{1,0:T(8,128)(2,1)S(1)}, bf16[384,128]{1,0:T(8,128)(2,1)}, u32[]{:S(2)}) copy-start(bf16[384,128]{1,0:T(8,128)(2,1)} %constant.23.clone.refs_9_) | copy-start | bytes 294916
  12.1 0.9 %copy-start.12 = (bf16[144,192]{1,0:T(8,128)(2,1)S(1)}, bf16[144,192]{1,0:T(8,128)(2,1)}, u32[]{:S(2)}) copy-start(bf16[144,192]{1,0:T(8,128)(2,1)} %constant.27.clone.refs_13_) | copy-start | bytes 165892
  13.0 0.7 %copy-start.14 = (f32[192]{0:T(256)S(1)}, f32[192]{0:T(256)}, u32[]{:S(2)}) copy-start(f32[192]{0:T(256)} %param.22) | copy-start | bytes 2308
  13.6 0.7 %copy-start.15 = (f32[192]{0:T(256)S(1)}, f32[192]{0:T(256)}, u32[]{:S(2)}) copy-start(f32[192]{0:T(256)} %param.23) | copy-start | bytes 2308
  14.3 0.7 %copy-start.16 = (f32[192]{0:T(256)S(1)}, f32[192]{0:T(256)}, u32[]{:S(2)}) copy-start(f32[192]{0:T(256)} %param.25) | copy-start | bytes 2308

commit v2 on v1

v2 whole, which is shorter than its diff:
```python
import functools

import jax
import jax.numpy as jnp
import ml_dtypes
import numpy as np
from jax import lax
from jax.experimental import pallas as pl
from jax.experimental.pallas import tpu as pltpu
from jax.sharding import PartitionSpec as P

HEADS = 6
D = 192
WLAT = 6
WLON = 12
ROWS = 6
COLS = 24
REL = 3312
SPAN = 2 * WLON - 1
FLAT = SPAN * WLAT * WLAT
EPSILON = 1e-05
SCALE = 32 ** (-0.5)
TOK = ROWS * COLS
WTOK = 96
BOTH = 2 * WTOK
FWD = ((0, 336), (336, 112), (448, 336), (784, 112))
FWD_ROWS = 896
FWD_CUT = (176, 64)
RET = ((0, 96), (96, 32), (128, 96), (224, 32))
RET_ROWS = 256
LANES = HEADS * 128
WIDE = 896
MASKED = -1e30
MESH = pl.DeviceIdType.MESH


def constants():
    def token(row, col):
        return row * COLS + col

    def wrow(rolled_row, rolled_col):
        return (rolled_col // WLON) * WTOK + (rolled_col % WLON) * 8 + rolled_row

    groups = [
        [
            (token(r, c), wrow((r + 3) % ROWS, (c + 18) % COLS))
            for r in rows
            for c in cols
        ]
        for rows in (range(3, ROWS), range(3))
        for cols in (range(6, COLS), range(6))
    ]

    pack = np.zeros((FWD_ROWS, 6 * TOK), np.float32)
    take_remote = np.zeros((2, 3 * BOTH, 480), np.float32)
    ret_pack = np.zeros((RET_ROWS, 3 * BOTH), np.float32)
    put_remote = np.zeros((3 * TOK, RET_ROWS), np.float32)
    for quarter, ((at, _), (back, _), group) in enumerate(zip(FWD, RET, groups)):
        n = len(group)
        for k, (t, w) in enumerate(group):
            for p in range(2):
                for part in range(3):
                    row = (3 * p + part) * n + k
                    pack[at + row, (3 * p + part) * TOK + t] = 1
                    seen = row - p * (FWD_CUT[quarter % 2] - 16)
                    take_remote[p, part * BOTH + w, (0, 176, 240, 416)[quarter] + seen] = 1
            ret_pack[back + k, w] = 1
            put_remote[t, back + k] = 1
            high = k >= n // 2
            slot = back + n + k % (n // 2)
            ret_pack[slot, (2 if high else 1) * BOTH + w] = 1
            put_remote[(2 if high else 1) * TOK + t, slot] = 1
    tails = np.zeros((2, D, 128), np.float32)
    for i in range(64):
        tails[0, 128 + i, i] = 1
        tails[1, 128 + i, 64 + i] = 1
    spread = np.zeros((256, WIDE), np.float32)
    for d in range(SPAN):
        for a in range(WLAT):
            spread[8 * d + a, SPAN * WLAT * a + d] = 1
    qkv_pad = np.zeros((3 * D, LANES), np.float32)
    for part in range(3):
        for i in range(D):
            qkv_pad[part * D + i, part * 256 + i] = 1
    proj_pad = np.zeros((D, 256), np.float32)
    for i in range(D):
        proj_pad[i, i if i < 128 else 64 + i] = 1
    head_mask = np.zeros((16, 256), np.float32)
    for h in range(HEADS):
        head_mask[h, h * 32 : (h + 1) * 32] = 1
    matrices = (
        pack,
        tails.reshape(2 * D, 128),
        take_remote.reshape(6 * BOTH, 480),
        ret_pack,
        put_remote,
        spread,
        qkv_pad,
        proj_pad,
        head_mask,
    )
    return tuple(m.astype(ml_dtypes.bfloat16) for m in matrices)


def dot(a, b):
    return jnp.dot(a, b, preferred_element_type=jnp.float32)


def dot_nt(a, b):
    return lax.dot_general(a, b, (((1,), (1,)), ((), ())), preferred_element_type=jnp.float32)


def dot_tn(a, b):
    return lax.dot_general(a, b, (((0,), (0,)), ((), ())), preferred_element_type=jnp.float32)


def low(a):
    return a.astype(jnp.bfloat16)


def kernel(n_lon, n_lat, n_in, *refs):
    ins, refs = refs[:n_in], refs[n_in:]
    (grad_out, table_out), refs = refs[:2], refs[2:]
    held, refs = refs[:n_in], refs[n_in:]
    (
        send_buf,
        recv_buf,
        ret_send,
        ret_recv,
        bias,
        table_pad,
        fold_buf,
        vecs,
        w_qkv,
        w_proj,
        q_heads,
        u_heads,
        red_src,
        red_in,
        z_slots,
        all_slots,
        in_sem,
        fwd_send,
        fwd_recv,
        back_send,
        back_recv,
        red_send,
        red_recv,
        z_send,
        z_recv,
        all_send,
        all_recv,
        ready,
    ) = refs
    (
        latent,
        out_grad,
        gain,
        shift,
        qkv_weight,
        query_bias,
        proj_weight,
        bias_table,
        pack,
        tails,
        take_remote,
        ret_pack,
        put_remote,
        spread,
        qkv_pad,
        proj_pad,
        head_mask,
    ) = held

    lon, lat = lax.axis_index("lon"), lax.axis_index("lat")
    lon_m = lax.rem(lon + n_lon - 1, n_lon)
    lat_m, lat_p = lax.rem(lat + n_lat - 1, n_lat), lax.rem(lat + 1, n_lat)

    def at(lon_at, lat_at):
        return {"lon": lon_at, "lat": lat_at}

    def half_way(strip):
        return (strip // 16) * 16 + lax.rem(strip + 8, 16)

    job = half_way(lon)
    job_p = lax.rem(job + 1, n_lon)
    workers = (
        at(half_way(lon), lat),
        at(half_way(lon_m), lat),
        at(half_way(lon), lat_m),
        at(half_way(lon_m), lat_m),
    )
    homes = (at(job, lat), at(job_p, lat), at(job, lat_p), at(job_p, lat_p))
    z_me = lax.rem(lon // 2, 8)
    y_me = lon // 16
    plane_me = y_me * 2 + lax.rem(lon, 2)

    def plane_peer(step):
        rank = lax.rem(plane_me + step, 8)
        return rank, at(((rank // 2) * 8 + z_me) * 2 + lax.rem(rank, 2), lat)

    def z_peer(step):
        z = lax.rem(z_me + step, 8)
        return at((y_me * 8 + z) * 2 + lax.rem(lon, 2), lat)

    z_ring = lax.rem(lat, 2) * 8 + z_me

    def ring_peer(step):
        z = lax.rem(z_ring + step + 16, 16)
        return at((y_me * 8 + lax.rem(z, 8)) * 2 + lax.rem(lon, 2), (lat // 2) * 2 + z // 8)

    barrier = pltpu.get_barrier_semaphore()
    everyone = list(workers) + list(homes)
    everyone += [ring_peer(s) for s in range(-4, 5) if s] + [plane_peer(s)[1] for s in range(1, 8)]
    for peer in everyone:
        pl.semaphore_signal(barrier, inc=1, device_id=peer, device_id_type=MESH)

    loads = [pltpu.make_async_copy(s, d, in_sem.at[i]) for i, (s, d) in enumerate(zip(ins, held))]
    order = [0, 1, 9, 8, 4, 14, 6, 15, 13, 7, 2, 3, 5, 16, 10, 11, 12]
    for i in order:
        loads[i].start()
    for i in (0, 1, 9, 8):
        loads[i].wait()

    source = []
    for p in range(2):
        rows = pl.ds((1 - p) * TOK, TOK)
        mixed = dot(latent[rows, :], tails[0:D, :]) + dot(out_grad[rows, :], tails[D : 2 * D, :])
        source += [latent[rows, 0:128], out_grad[rows, 0:128], low(mixed)]
    send_buf[...] = low(dot(pack[...], jnp.concatenate(source, 0)))

    pl.semaphore_wait(barrier, len(everyone))
    for step in (-4, 4):
        pl.semaphore_signal(ready, inc=1, device_id=ring_peer(step), device_id_type=MESH)
    upper = lax.rem(lat, 2)

    def pick(k, places):
        here, there = places[k], places[(k + 2) % 4]
        return {name: jnp.where(upper == 0, here[name], there[name]) for name in here}

    def forward(p, k, moved):
        q = lax.rem(k + 2 * upper, 4) if moved else k
        cut = FWD_CUT[k % 2]
        size = cut if p == 0 else FWD[k][1] - cut
        start = pl.multiple_of((q // 2) * FWD[2][0] + FWD[k % 2][0] + p * cut, 16)
        return pltpu.make_async_remote_copy(
            src_ref=send_buf.at[pl.ds(start, size)],
            dst_ref=recv_buf.at[pl.ds(start, size)],
            send_sem=fwd_send.at[p, q],
            recv_sem=fwd_recv.at[p, q],
            device_id=pick(k, workers) if moved else workers[k],
            device_id_type=MESH,
        )

    def backward(p, k, moved):
        q = lax.rem(k + 2 * upper, 4) if moved else k
        start = pl.multiple_of((q // 2) * RET[2][0] + RET[k % 2][0], 16)
        return pltpu.make_async_remote_copy(
            src_ref=ret_send.at[p, pl.ds(start, RET[k][1])],
            dst_ref=ret_recv.at[p, pl.ds(start, RET[k][1])],
            send_sem=back_send.at[p, q],
            recv_sem=back_recv.at[p, q],
            device_id=pick(k, homes) if moved else homes[k],
            device_id_type=MESH,
        )

    for ks in ((0, 1), (2, 3)):
        for p in range(2):
            for k in ks:
                forward(p, k, True).start()

    for i in order:
        if i not in (0, 1, 9, 8):
            loads[i].wait()

    w_qkv[0:D, :] = low(dot(qkv_weight[...], qkv_pad[...]))
    w_qkv[D:256, :] = jnp.zeros((256 - D, LANES), jnp.bfloat16)
    w_proj[0:D, :] = low(dot(proj_weight[...], proj_pad[...]))
    w_proj[D:256, :] = jnp.zeros((256 - D, 256), jnp.bfloat16)
    vecs[...] = jnp.zeros((8, 256), jnp.float32)
    vecs[0:1, 0:D] = gain[...]
    vecs[1:2, 0:D] = shift[...]
    vecs[2:3, 0:D] = query_bias[...]
    for h in range(HEADS):
        pad = pl.ds(h * 128 + WTOK, 128 - WTOK)
        q_heads[:, pad, :] = jnp.zeros((4, 128 - WTOK, 256), jnp.bfloat16)
        u_heads[:, pad, :] = jnp.zeros((4, 128 - WTOK, 256), jnp.bfloat16)

    lane8 = lax.broadcasted_iota(jnp.int32, (8, 128), 1)
    row8 = lax.broadcasted_iota(jnp.int32, (8, 128), 0)
    last = (lat == n_lat - 1).astype(jnp.int32)
    query_half = (lax.rem(lane8, 8) >= 3).astype(jnp.int32)
    key_half = (row8 >= 3).astype(jnp.int32)
    left_out = (row8 >= WLAT).astype(jnp.int32) + last * (query_half ^ key_half) > 0

    for p in range(2):
        table_pad[...] = jnp.zeros((8, WIDE), jnp.float32)
        if p == 0:
            for h in range(HEADS):
                table_pad[h : h + 1, :] = bias_table[h, :, 0:WIDE]
        else:
            for h in range(HEADS):
                table_pad[h : h + 1, 0 : REL - 2432] = bias_table[h, :, 2432:REL]
        entries = table_pad[...]
        for b in range(8):
            if b < WLAT:
                moved = pltpu.roll(entries, (2 * WIDE - SPAN * b - 52 * p) % WIDE, 1)
                top = low(moved)
                rest = low(moved - top.astype(jnp.float32))
                row = dot_nt(top, spread[...]) + dot_nt(rest, spread[...])
            else:
                row = jnp.zeros((8, 256), jnp.float32)
            fold_buf[0, 8 * b : 8 * b + 8, :] = row[:, 0:128]
            fold_buf[1, 8 * b : 8 * b + 8, :] = row[:, 128:256]
        for h in range(HEADS):
            near = fold_buf[0, pl.ds(h, 8, stride=8), :]
            far = fold_buf[1, pl.ds(h, 8, stride=8), :]
            for r in range(WLON):
                s = 8 * (WLON - 1 - r)
                if s:
                    block = pltpu.roll(jnp.where(lane8 >= s, near, far), 128 - s, 1)
                else:
                    block = near
                bias[p, 8 * r : 8 * r + 8, 128 * h : 128 * h + 128] = jnp.where(left_out, MASKED, block)

    gain_w, shift_w, query_w = vecs[0:1, :], vecs[1:2, :], vecs[2:3, :]
    below64 = lax.broadcasted_iota(jnp.int32, (BOTH, 128), 1) < 64
    low_lane = lax.broadcasted_iota(jnp.int32, (BOTH, 256), 1) < D
    flats = []
    kept = []

    def send_back(p):
        per_window, normed, inverse = kept[p]
        rows = []
        for w, (prob_low, score_low, key_w) in enumerate(per_window):
            value_g = dot(prob_low, u_heads[2 * p + w])
            key_g = dot(score_low, q_heads[2 * p + w]) * SCALE
            query_all = dot_tn(score_low, key_w)
            query_g = None
            for h in range(HEADS):
                term = query_all[h * 128 : h * 128 + WTOK] * head_mask[h : h + 1, :].astype(jnp.float32)
                query_g = term if query_g is None else query_g + term
            rows.append(jnp.concatenate([low(query_g * SCALE), low(key_g), low(value_g)], 1))
        hidden_grad = dot_nt(jnp.concatenate(rows, 0), w_qkv[...])
        scaled = hidden_grad * gain_w
        mean_g = jnp.sum(scaled, 1, keepdims=True) * (1.0 / D)
        mean_gn = jnp.sum(scaled * normed, 1, keepdims=True) * (1.0 / D)
        branch = jnp.where(low_lane, inverse * (scaled - mean_g - normed * mean_gn), 0.0)
        second = branch[:, 128:256]
        stacked = jnp.concatenate([branch[:, 0:128], second, pltpu.roll(second, 64, 1)], 0)
        ret_send[p] = low(dot(ret_pack[...], low(stacked)))
        for k in range(2):
            backward(p, k, True).start()


    for p in range(2):
        for k in range(4):
            forward(p, k, False).wait_recv()
        got = [
            recv_buf[pl.ds(FWD[k][0] + p * (FWD_CUT[k % 2] - 16), FWD_CUT[k % 2]), :] for k in range(4)
        ]
        tokens = dot(take_remote[pl.ds(3 * BOTH * p, 3 * BOTH), :], jnp.concatenate(got, 0))
        x_a, x_b, x_c = tokens[0:BOTH], tokens[BOTH : 2 * BOTH], tokens[2 * BOTH :]
        tail = jnp.where(below64, x_c, 0.0)
        center = (jnp.sum(x_a, 1, keepdims=True) + jnp.sum(tail, 1, keepdims=True)) * (1.0 / D)
        c_a = x_a - center
        c_t = jnp.where(below64, x_c - center, 0.0)
        spread_sq = (
            jnp.sum(c_a * c_a, 1, keepdims=True) + jnp.sum(c_t * c_t, 1, keepdims=True)
        ) * (1.0 / D)
        inverse = lax.rsqrt(spread_sq + EPSILON)
        normed = jnp.concatenate([c_a, c_t], 1) * inverse
        hidden = low(normed * gain_w + shift_w)
        projected = dot(hidden, w_qkv[...])
        queries = low(projected[:, 0:256] + query_w)
        keys = low(projected[:, 256:512])
        values = low(projected[:, 512:768])
        incoming = low(jnp.concatenate([x_b, x_c], 1))
        upstream = low(dot_nt(incoming, w_proj[...]))

        per_window = []
        score_sum = None
        for w in range(2):
            span = slice(w * WTOK, (w + 1) * WTOK)
            q_w, u_w = q_heads.at[2 * p + w], u_heads.at[2 * p + w]
            for h in range(HEADS):
                mask = head_mask[h : h + 1, :]
                q_w[pl.ds(h * 128, WTOK), :] = queries[span] * mask
                u_w[pl.ds(h * 128, WTOK), :] = upstream[span] * mask
            scores = dot_nt(keys[span], q_w[...]) * SCALE + bias[p]
            weights = jnp.exp(scores)
            probs = weights * (1.0 / jnp.sum(weights, 0, keepdims=True))
            prob_grad = dot_nt(values[span], u_w[...])
            inner = jnp.sum(probs * prob_grad, 0, keepdims=True)
            score_grad = probs * (prob_grad - inner)
            score_sum = score_grad if score_sum is None else score_sum + score_grad
            per_window.append((low(probs), low(score_grad), keys[span]))
        kept.append((per_window, normed, inverse))

        for h in range(HEADS):
            near = far = None
            for r in range(WLON):
                s = 8 * (WLON - 1 - r)
                block = score_sum[8 * r : 8 * r + 8, 128 * h : 128 * h + 128]
                if s:
                    block = pltpu.roll(block, s, 1)
                    wrapped = jnp.where(lane8 < s, block, 0.0)
                    block = jnp.where(lane8 < s, 0.0, block)
                    far = wrapped if far is None else far + wrapped
                near = block if near is None else near + block
            fold_buf[0, 8 * h : 8 * h + 8, :] = near
            fold_buf[1, 8 * h : 8 * h + 8, :] = far
        by_row = [
            jnp.concatenate([fold_buf[part, pl.ds(b, 8, stride=8), :] for part in range(2)], 1)
            for b in range(WLAT)
        ]
        lines = dot(low(jnp.concatenate(by_row, 0)), spread[...])
        flat = None
        for b in range(WLAT):
            line = lines[8 * b : 8 * b + 8]
            if b or p:
                line = pltpu.roll(line, SPAN * b + 52 * p, 1)
            flat = line if flat is None else flat + line
        flats.append(flat)
        if p == 0:
            send_back(0)

    for c in range(8):
        for half in range(2):
            tile = 2 * c + half
            if tile < 14:
                part = flats[tile // 7][:, 128 * (tile % 7) : 128 * (tile % 7) + 128]
            else:
                part = jnp.zeros((8, 128), jnp.float32)
            all_slots[c, 8 * half : 8 * half + 8, :] = part
        red_src[c] = low(all_slots[c])
    reduced = []
    for s in range(1, 8):
        rank, peer = plane_peer(s)
        copy = pltpu.make_async_remote_copy(
            src_ref=red_src.at[rank],
            dst_ref=red_in.at[s - 1],
            send_sem=red_send.at[s - 1],
            recv_sem=red_recv.at[s - 1],
            device_id=peer,
            device_id_type=MESH,
        )
        copy.start()
        reduced.append(copy)

    send_back(1)
    for copy in reduced:
        copy.wait_recv()
    total = red_src[plane_me].astype(jnp.float32)
    for s in range(7):
        total = total + red_in[s].astype(jnp.float32)
    z_slots[z_me] = low(total)
    pl.semaphore_wait(ready, 2)
    along = []
    for s in range(1, 8):
        copy = pltpu.make_async_remote_copy(
            src_ref=z_slots.at[z_me],
            dst_ref=z_slots.at[z_me],
            send_sem=z_send.at[s - 1],
            recv_sem=z_recv.at[s - 1],
            device_id=z_peer(s),
            device_id_type=MESH,
        )
        copy.start()
        along.append(copy)

    for p in range(2):
        for k in range(2, 4):
            backward(p, k, True).start()

    for copy in along:
        copy.wait_recv()
    total = z_slots[0].astype(jnp.float32)
    for z in range(1, 8):
        total = total + z_slots[z].astype(jnp.float32)
    all_slots[plane_me] = total
    gathered = []
    for s in range(1, 8):
        _, peer = plane_peer(s)
        copy = pltpu.make_async_remote_copy(
            src_ref=all_slots.at[plane_me],
            dst_ref=all_slots.at[plane_me],
            send_sem=all_send.at[s - 1],
            recv_sem=all_recv.at[s - 1],
            device_id=peer,
            device_id_type=MESH,
        )
        copy.start()
        gathered.append(copy)

    for p in range(2):
        rows = pl.ds((1 - p) * TOK, TOK)
        for k in range(4):
            backward(p, k, False).wait_recv()
        got = dot(put_remote[...], ret_recv[p])
        rest = got[TOK : 2 * TOK] + pltpu.roll(got[2 * TOK :], 64, 1)
        grad_out[rows, 0:128] = low(out_grad[rows, 0:128].astype(jnp.float32) + got[0:TOK])
        grad_out[rows, 128:D] = low(out_grad[rows, 128:D].astype(jnp.float32) + rest[:, 0 : D - 128])

    table_out[...] = jnp.zeros((HEADS, 1, REL), jnp.float32)
    for copy in gathered:
        copy.wait_recv()
    for tile in range(14):
        start = 128 * tile if tile < 7 else 2432 + 128 * (tile - 7)
        size = min(128, REL - start)
        for h in range(HEADS):
            entries = all_slots[tile // 2, pl.ds(8 * (tile % 2) + h, 1), :]
            table_out[h, :, start : start + size] = entries[:, 0:size]

    for p in range(2):
        for k in range(4):
            forward(p, k, False).wait_send()
            backward(p, k, False).wait_send()
    for copy in reduced + along + gathered:
        copy.wait_send()


def local(n_lon, n_lat, latent, out_grad, gain, shift, qkv_weight, query_bias, proj_weight, bias_table, band_rows):
    del band_rows
    consts = [jnp.asarray(c) for c in constants()]
    args = [
        latent.reshape(2 * TOK, D),
        out_grad.reshape(2 * TOK, D),
        gain.reshape(1, D),
        shift.reshape(1, D),
        qkv_weight,
        query_bias.reshape(1, D),
        proj_weight,
        bias_table.reshape(HEADS, 1, REL),
    ] + consts
    bf16, f32 = jnp.bfloat16, jnp.float32
    dma = pltpu.SemaphoreType.DMA
    scratch = [pltpu.VMEM(a.shape, a.dtype) for a in args] + [
        pltpu.VMEM((FWD_ROWS, 128), bf16),
        pltpu.VMEM((FWD_ROWS, 128), bf16),
        pltpu.VMEM((2, RET_ROWS, 128), bf16),
        pltpu.VMEM((2, RET_ROWS, 128), bf16),
        pltpu.VMEM((2, WTOK, LANES), f32),
        pltpu.VMEM((8, WIDE), f32),
        pltpu.VMEM((2, 64, 128), f32),
        pltpu.VMEM((8, 256), f32),
        pltpu.VMEM((256, LANES), bf16),
        pltpu.VMEM((256, 256), bf16),
        pltpu.VMEM((4, LANES, 256), bf16),
        pltpu.VMEM((4, LANES, 256), bf16),
        pltpu.VMEM((8, 16, 128), bf16),
        pltpu.VMEM((7, 16, 128), bf16),
        pltpu.VMEM((8, 16, 128), bf16),
        pltpu.VMEM((8, 16, 128), f32),
        dma((len(args),)),
        dma((2, 4)),
        dma((2, 4)),
        dma((2, 4)),
        dma((2, 4)),
        dma((7,)),
        dma((7,)),
        dma((7,)),
        dma((7,)),
        dma((7,)),
        dma((7,)),
        pltpu.SemaphoreType.REGULAR,
    ]
    grad, table = pl.pallas_call(
        functools.partial(kernel, n_lon, n_lat, len(args)),
        out_shape=(
            jax.ShapeDtypeStruct((2 * TOK, D), bf16),
            jax.ShapeDtypeStruct((HEADS, 1, REL), f32),
        ),
        in_specs=[pl.BlockSpec(memory_space=pltpu.HBM)] * len(args),
        out_specs=(pl.BlockSpec(memory_space=pltpu.VMEM), pl.BlockSpec(memory_space=pltpu.VMEM)),
        scratch_shapes=scratch,
        compiler_params=pltpu.CompilerParams(
            collective_id=0, has_side_effects=True, vmem_limit_bytes=63 * 1024 * 1024
        ),
    )(*args)
    return grad.reshape(latent.shape), table.reshape(bias_table.shape)


def solution(mesh):
    in_specs = (
        P(None, "lat", "lon", None),
        P(None, "lat", "lon", None),
        P(),
        P(),
        P(),
        P(),
        P(),
        P("lat", None, None, None),
        P("lat"),
    )
    out_specs = (P(None, "lat", "lon", None), P("lat", None, None, None))
    body = functools.partial(local, mesh.shape["lon"], mesh.shape["lat"])
    return jax.shard_map(body, mesh=mesh, in_specs=in_specs, out_specs=out_specs, check_vma=False)
```

time: 66.3 us -> 49.7 us (0.75)
  local copies, waits for them, and re-layouts: 15.7 us -> 3.11 us
  Pallas kernels: 49.3 us -> 45.8 us
    unnamed x37 -> x2, local copies, waits for them, and re-layouts: 15.7 us -> 3.11 us
    pallas_call x1, Pallas kernels: 49.3 us -> 45.8 us  [local(): pl.pallas_call(functools.partial(kernel, n_lon, n_lat, len(args)), out_sh...]
where the time goes in v2:
time: 49.7 us; the launch traced here: 49.5 us
  Pallas kernels  45.8 us (92%)
  local copies, waits for them, and re-layouts  3.11 us (6%)
  between operations  0.64 us (1%)
    pallas_call x1, Pallas kernels, local(): pl.pallas_call(functools.partial(kernel, n_lon, n_lat, len(args)), out_sh...  45.8 us
    unnamed x2, local copies, waits for them, and re-layouts  3.11 us

profile of v2, /device:TPU:1, one launch (start us, length us, event | category | flops | bytes accessed | tf_op | source)
XLA Modules:
  0.0 49.5 jit_solution(8522749408958493597)
XLA Ops:
  0.6 45.8 %shard_map.176 = (bf16[288,192]{1,0:T(8,128)(2,1)}, f32[6,1,3312]{2,1,0:T(1,128)}) custom-call(bf16[288,192]{1,0:T(8,128)(2,1)} %bitcast.10, bf16[288,192]{1,0:T(8,128)(2,1)} %bitcast.11, f32[1,192]{1,0:T(1,128)} %bitcast.15, f32[1,192]{1,0:T(1,128)} %bitcast.16, bf16[192,576]{1,0:T(8,128)(2,1)} %refs_4_.1, f32[1,192]{1,0:T(1,128)} %bitcast.17, ...), custom_call_target="tpu_custom_call" | custom-call | tf_op jit(solution)/shard_map/pallas_call | solution.py:568
  46.4 1.6 %copy.22 = bf16[2,6,24,192]{3,2,1,0:T(8,128)(2,1)} copy(bf16[2,6,24,192]{3,2,1,0:T(8,128)(2,1)} %bitcast.12) | data formatting | bytes 221184
  48.0 1.5 %copy.23 = f32[1,1,6,3312]{3,1,2,0:T(1,128)} copy(f32[1,1,6,3312]{3,1,2,0:T(1,128)} %bitcast.14) | data formatting | bytes 158976

commit v3 on v2

--- a/solution.py
+++ b/solution.py
@@ -120,7 +120,7 @@
 
 def kernel(n_lon, n_lat, n_in, *refs):
     ins, refs = refs[:n_in], refs[n_in:]
-    (grad_out, table_out), refs = refs[:2], refs[2:]
+    (grad_out, all_slots), refs = refs[:2], refs[2:]
     held, refs = refs[:n_in], refs[n_in:]
     (
         send_buf,
@@ -138,7 +138,9 @@
         red_src,
         red_in,
         z_slots,
-        all_slots,
+        final,
+        grad_held,
+        out_sem,
         in_sem,
         fwd_send,
         fwd_recv,
@@ -425,15 +427,10 @@
         if p == 0:
             send_back(0)
 
+    tiles = [flats[p][:, 128 * k : 128 * k + 128] for p in range(2) for k in range(7)]
+    tiles += [jnp.zeros((8, 128), jnp.float32)] * 2
     for c in range(8):
-        for half in range(2):
-            tile = 2 * c + half
-            if tile < 14:
-                part = flats[tile // 7][:, 128 * (tile % 7) : 128 * (tile % 7) + 128]
-            else:
-                part = jnp.zeros((8, 128), jnp.float32)
-            all_slots[c, 8 * half : 8 * half + 8, :] = part
-        red_src[c] = low(all_slots[c])
+        red_src[c] = low(jnp.concatenate(tiles[2 * c : 2 * c + 2], 0))
     reduced = []
     for s in range(1, 8):
         rank, peer = plane_peer(s)
@@ -478,12 +475,14 @@
     total = z_slots[0].astype(jnp.float32)
     for z in range(1, 8):
         total = total + z_slots[z].astype(jnp.float32)
-    all_slots[plane_me] = total
+    final[...] = total
+    own_slot = pltpu.make_async_copy(final, all_slots.at[plane_me], out_sem.at[2])
+    own_slot.start()
     gathered = []
     for s in range(1, 8):
         _, peer = plane_peer(s)
         copy = pltpu.make_async_remote_copy(
-            src_ref=all_slots.at[plane_me],
+            src_ref=final,
             dst_ref=all_slots.at[plane_me],
             send_sem=all_send.at[s - 1],
             recv_sem=all_recv.at[s - 1],
@@ -493,31 +492,56 @@
         copy.start()
         gathered.append(copy)
 
+    written = []
     for p in range(2):
         rows = pl.ds((1 - p) * TOK, TOK)
         for k in range(4):
             backward(p, k, False).wait_recv()
         got = dot(put_remote[...], ret_recv[p])
         rest = got[TOK : 2 * TOK] + pltpu.roll(got[2 * TOK :], 64, 1)
-        grad_out[rows, 0:128] = low(out_grad[rows, 0:128].astype(jnp.float32) + got[0:TOK])
-        grad_out[rows, 128:D] = low(out_grad[rows, 128:D].astype(jnp.float32) + rest[:, 0 : D - 128])
-
-    table_out[...] = jnp.zeros((HEADS, 1, REL), jnp.float32)
+        grad_held[rows, 0:128] = low(out_grad[rows, 0:128].astype(jnp.float32) + got[0:TOK])
+        grad_held[rows, 128:D] = low(out_grad[rows, 128:D].astype(jnp.float32) + rest[:, 0 : D - 128])
+        copy = pltpu.make_async_copy(grad_held.at[rows], grad_out.at[rows], out_sem.at[p])
+        copy.start()
+        written.append(copy)
+
     for copy in gathered:
         copy.wait_recv()
-    for tile in range(14):
-        start = 128 * tile if tile < 7 else 2432 + 128 * (tile - 7)
-        size = min(128, REL - start)
-        for h in range(HEADS):
-            entries = all_slots[tile // 2, pl.ds(8 * (tile % 2) + h, 1), :]
-            table_out[h, :, start : start + size] = entries[:, 0:size]
-
+    for copy in written + [own_slot]:
+        copy.wait()
     for p in range(2):
         for k in range(4):
             forward(p, k, False).wait_send()
             backward(p, k, False).wait_send()
     for copy in reduced + along + gathered:
         copy.wait_send()
+
+
+def hand_over(grad, slots, grad_out, table_out, grad_held, slots_held, table_held, sems):
+    read_slots = pltpu.make_async_copy(slots, slots_held, sems.at[0, 3])
+    read_slots.start()
+    reads, writes = [], []
+    for i in range(3):
+        rows = pl.ds(96 * i, 96)
+        reads.append(pltpu.make_async_copy(grad.at[rows], grad_held.at[rows], sems.at[0, i]))
+        writes.append(pltpu.make_async_copy(grad_held.at[rows], grad_out.at[rows], sems.at[1, i]))
+    for copy in reads:
+        copy.start()
+    table_held[...] = jnp.zeros((HEADS, 1, REL), jnp.float32)
+    read_slots.wait()
+    for tile in range(14):
+        start = 128 * tile if tile < 7 else 2432 + 128 * (tile - 7)
+        size = min(128, REL - start)
+        for h in range(HEADS):
+            entries = slots_held[tile // 2, pl.ds(8 * (tile % 2) + h, 1), :]
+            table_held[h, :, start : start + size] = entries[:, 0:size]
+    write_table = pltpu.make_async_copy(table_held, table_out, sems.at[1, 3])
+    write_table.start()
+    for read, write in zip(reads, writes):
+        read.wait()
+        write.start()
+    for copy in writes + [write_table]:
+        copy.wait()
 
 
 def local(n_lon, n_lat, latent, out_grad, gain, shift, qkv_weight, query_bias, proj_weight, bias_table, band_rows):
@@ -551,7 +575,9 @@
         pltpu.VMEM((8, 16, 128), bf16),
         pltpu.VMEM((7, 16, 128), bf16),
         pltpu.VMEM((8, 16, 128), bf16),
-        pltpu.VMEM((8, 16, 128), f32),
+        pltpu.VMEM((16, 128), f32),
+        pltpu.VMEM((2 * TOK, D), bf16),
+        dma((3,)),
         dma((len(args),)),
         dma((2, 4)),
         dma((2, 4)),
@@ -565,19 +591,35 @@
         dma((7,)),
         pltpu.SemaphoreType.REGULAR,
     ]
-    grad, table = pl.pallas_call(
+    grad, slots = pl.pallas_call(
         functools.partial(kernel, n_lon, n_lat, len(args)),
         out_shape=(
             jax.ShapeDtypeStruct((2 * TOK, D), bf16),
-            jax.ShapeDtypeStruct((HEADS, 1, REL), f32),
+            jax.ShapeDtypeStruct((8, 16, 128), f32),
         ),
         in_specs=[pl.BlockSpec(memory_space=pltpu.HBM)] * len(args),
-        out_specs=(pl.BlockSpec(memory_space=pltpu.VMEM), pl.BlockSpec(memory_space=pltpu.VMEM)),
+        out_specs=(pl.BlockSpec(memory_space=pltpu.HBM), pl.BlockSpec(memory_space=pltpu.HBM)),
         scratch_shapes=scratch,
         compiler_params=pltpu.CompilerParams(
             collective_id=0, has_side_effects=True, vmem_limit_bytes=63 * 1024 * 1024
         ),
     )(*args)
+    grad, table = pl.pallas_call(
+        hand_over,
+        out_shape=(
+            jax.ShapeDtypeStruct((2 * TOK, D), bf16),
+            jax.ShapeDtypeStruct((HEADS, 1, REL), f32),
+        ),
+        in_specs=[pl.BlockSpec(memory_space=pltpu.HBM)] * 2,
+        out_specs=(pl.BlockSpec(memory_space=pltpu.HBM), pl.BlockSpec(memory_space=pltpu.HBM)),
+        scratch_shapes=[
+            pltpu.VMEM((2 * TOK, D), bf16),
+            pltpu.VMEM((8, 16, 128), f32),
+            pltpu.VMEM((HEADS, 1, REL), f32),
+            dma((2, 4)),
+        ],
+        compiler_params=pltpu.CompilerParams(vmem_limit_bytes=63 * 1024 * 1024),
+    )(grad, slots)
     return grad.reshape(latent.shape), table.reshape(bias_table.shape)
 
 

time: 49.7 us -> 47.6 us (0.958)
  local copies, waits for them, and re-layouts: 3.11 us -> 0 us
  Pallas kernels: 45.8 us -> 46.8 us
    unnamed x2 -> x0, local copies, waits for them, and re-layouts: 3.11 us -> none
    pallas_call x0 -> x1, Pallas kernels: none -> 1.62 us  [local(): pl.pallas_call(hand_over, out_shape=(jax.ShapeDtypeStruct((2 * TOK, D), b...]
    pallas_call x1, Pallas kernels: 45.8 us -> 45.1 us  [local(): pl.pallas_call(functools.partial(kernel, n_lon, n_lat, len(args)), out_sh...]
where the time goes in v3:
time: 47.6 us; the launch traced here: 47.4 us
  Pallas kernels  46.8 us (98%)
  between operations  0.64 us (1%)
    pallas_call x1, Pallas kernels, local(): pl.pallas_call(functools.partial(kernel, n_lon, n_lat, len(args)), out_sh...  45.1 us
    pallas_call x1, Pallas kernels, local(): pl.pallas_call(hand_over, out_shape=(jax.ShapeDtypeStruct((2 * TOK, D), b...  1.62 us

profile of v3, /device:TPU:1, one launch (start us, length us, event | category | flops | bytes accessed | tf_op | source)
XLA Modules:
  0.0 47.4 jit_solution(13752795900676492061)
XLA Ops:
  0.6 45.1 %shard_map.176 = (bf16[288,192]{1,0:T(8,128)(2,1)}, f32[8,16,128]{2,1,0:T(8,128)}) custom-call(bf16[288,192]{1,0:T(8,128)(2,1)} %bitcast.10, bf16[288,192]{1,0:T(8,128)(2,1)} %bitcast.11, f32[1,192]{1,0:T(1,128)} %bitcast.13, f32[1,192]{1,0:T(1,128)} %bitcast.14, bf16[192,576]{1,0:T(8,128)(2,1)} %refs_4_.1, f32[1,192]{1,0:T(1,128)} %bitcast.15, ...), custom_call_target="tpu_custom_call" | custom-call | tf_op jit(solution)/shard_map/pallas_call | solution.py:594
  45.8 1.6 %shard_map.177 = (bf16[288,192]{1,0:T(8,128)(2,1)}, f32[6,1,3312]{2,1,0:T(1,128)}) custom-call(bf16[288,192]{1,0:T(8,128)(2,1)} %get-tuple-element.6.grad, f32[8,16,128]{2,1,0:T(8,128)} %get-tuple-element.7.slots), custom_call_target="tpu_custom_call" | custom-call | tf_op jit(solution)/shard_map/pallas_call | solution.py:607

commit v4 on v3

--- a/solution.py
+++ b/solution.py
@@ -25,7 +25,10 @@
 BOTH = 2 * WTOK
 FWD = ((0, 336), (336, 112), (448, 336), (784, 112))
 FWD_ROWS = 896
-FWD_CUT = (176, 64)
+FWD_WIDE = ((0, 112), (112, 64), (176, 96), (272, 64))
+FWD_NARROW = (None, (0, 64), None, (64, 48))
+SEEN_WIDE = ((0, 112), (96, 80), (160, 112), (256, 80))
+SEEN_NARROW = (None, (0, 64), None, (48, 64))
 RET = ((0, 96), (96, 32), (128, 96), (224, 32))
 RET_ROWS = 256
 LANES = HEADS * 128
@@ -44,26 +47,31 @@
     groups = [
         [
             (token(r, c), wrow((r + 3) % ROWS, (c + 18) % COLS))
+            for part in cols
             for r in rows
-            for c in cols
+            for c in part
         ]
         for rows in (range(3, ROWS), range(3))
-        for cols in (range(6, COLS), range(6))
+        for cols in ((range(6, 18), range(18, COLS)), (range(6),))
     ]
 
     pack = np.zeros((FWD_ROWS, 6 * TOK), np.float32)
-    take_remote = np.zeros((2, 3 * BOTH, 480), np.float32)
+    take_remote = np.zeros((4, 3 * WTOK, 288), np.float32)
     ret_pack = np.zeros((RET_ROWS, 3 * BOTH), np.float32)
     put_remote = np.zeros((3 * TOK, RET_ROWS), np.float32)
     for quarter, ((at, _), (back, _), group) in enumerate(zip(FWD, RET, groups)):
         n = len(group)
         for k, (t, w) in enumerate(group):
+            wide = quarter % 2 == 0
+            first, count, mine = (0, n, 1) if not wide else (0, 36, 0) if k < 36 else (36, 18, 1)
             for p in range(2):
+                stage = 2 * p + mine
+                seen_at = (SEEN_WIDE if wide else SEEN_NARROW)[stage][0]
+                column = (0, 80, 144, 224)[quarter] if mine else 56 * quarter
                 for part in range(3):
-                    row = (3 * p + part) * n + k
+                    row = 3 * (p * n + first) + part * count + k - first
                     pack[at + row, (3 * p + part) * TOK + t] = 1
-                    seen = row - p * (FWD_CUT[quarter % 2] - 16)
-                    take_remote[p, part * BOTH + w, (0, 176, 240, 416)[quarter] + seen] = 1
+                    take_remote[stage, part * WTOK + w % WTOK, column + row - seen_at] = 1
             ret_pack[back + k, w] = 1
             put_remote[t, back + k] = 1
             high = k >= n // 2
@@ -91,7 +99,7 @@
     matrices = (
         pack,
         tails.reshape(2 * D, 128),
-        take_remote.reshape(6 * BOTH, 480),
+        take_remote.reshape(12 * WTOK, 288),
         ret_pack,
         put_remote,
         spread,
@@ -152,6 +160,8 @@
         z_recv,
         all_send,
         all_recv,
+        row_held,
+        row_sem,
         ready,
     ) = refs
     (
@@ -176,7 +186,8 @@
 
     lon, lat = lax.axis_index("lon"), lax.axis_index("lat")
     lon_m = lax.rem(lon + n_lon - 1, n_lon)
-    lat_m, lat_p = lax.rem(lat + n_lat - 1, n_lat), lax.rem(lat + 1, n_lat)
+    lat_m = lax.rem(lat + n_lat - 1, n_lat)
+    two_on, two_back = lax.rem(lat + 2, n_lat), lax.rem(lat + n_lat - 2, n_lat)
 
     def at(lon_at, lat_at):
         return {"lon": lon_at, "lat": lat_at}
@@ -184,15 +195,22 @@
     def half_way(strip):
         return (strip // 16) * 16 + lax.rem(strip + 8, 16)
 
+    upper = lax.rem(lat, 2)
+
+    def lat_worker(band):
+        return lax.rem(band + 2 * lax.rem(band, 2), n_lat)
+
+    job_lat = lax.rem(lat + n_lat - 2 * upper, n_lat)
+    job_lat_p = lax.rem(job_lat + 1, n_lat)
     job = half_way(lon)
     job_p = lax.rem(job + 1, n_lon)
     workers = (
-        at(half_way(lon), lat),
-        at(half_way(lon_m), lat),
-        at(half_way(lon), lat_m),
-        at(half_way(lon_m), lat_m),
+        at(half_way(lon), lat_worker(lat)),
+        at(half_way(lon_m), lat_worker(lat)),
+        at(half_way(lon), lat_worker(lat_m)),
+        at(half_way(lon_m), lat_worker(lat_m)),
     )
-    homes = (at(job, lat), at(job_p, lat), at(job, lat_p), at(job_p, lat_p))
+    homes = (at(job, job_lat), at(job_p, job_lat), at(job, job_lat_p), at(job_p, job_lat_p))
     z_me = lax.rem(lon // 2, 8)
     y_me = lon // 16
     plane_me = y_me * 2 + lax.rem(lon, 2)
@@ -212,10 +230,15 @@
         return at((y_me * 8 + lax.rem(z, 8)) * 2 + lax.rem(lon, 2), (lat // 2) * 2 + z // 8)
 
     barrier = pltpu.get_barrier_semaphore()
-    everyone = list(workers) + list(homes)
-    everyone += [ring_peer(s) for s in range(-4, 5) if s] + [plane_peer(s)[1] for s in range(1, 8)]
+    everyone = list(homes[2:] + homes[:2])
+    everyone += [ring_peer(s) for s in range(-4, 5) if s]
+    everyone += [plane_peer(s)[1] for s in range(1, 8)]
     for peer in everyone:
         pl.semaphore_signal(barrier, inc=1, device_id=peer, device_id_type=MESH)
+
+    @pl.when(upper == 1)
+    def _():
+        pl.semaphore_signal(barrier, inc=1, device_id=at(lon, two_back), device_id_type=MESH)
 
     loads = [pltpu.make_async_copy(s, d, in_sem.at[i]) for i, (s, d) in enumerate(zip(ins, held))]
     order = [0, 1, 9, 8, 4, 14, 6, 15, 13, 7, 2, 3, 5, 16, 10, 11, 12]
@@ -231,25 +254,22 @@
         source += [latent[rows, 0:128], out_grad[rows, 0:128], low(mixed)]
     send_buf[...] = low(dot(pack[...], jnp.concatenate(source, 0)))
 
-    pl.semaphore_wait(barrier, len(everyone))
+    pl.semaphore_wait(barrier, len(everyone) + upper)
     for step in (-4, 4):
         pl.semaphore_signal(ready, inc=1, device_id=ring_peer(step), device_id_type=MESH)
-    upper = lax.rem(lat, 2)
-
     def pick(k, places):
         here, there = places[k], places[(k + 2) % 4]
         return {name: jnp.where(upper == 0, here[name], there[name]) for name in here}
 
-    def forward(p, k, moved):
+    def forward(stage, k, moved):
         q = lax.rem(k + 2 * upper, 4) if moved else k
-        cut = FWD_CUT[k % 2]
-        size = cut if p == 0 else FWD[k][1] - cut
-        start = pl.multiple_of((q // 2) * FWD[2][0] + FWD[k % 2][0] + p * cut, 16)
+        offset, size = (FWD_NARROW if k % 2 else FWD_WIDE)[stage]
+        start = pl.multiple_of((q // 2) * FWD[2][0] + FWD[k % 2][0] + offset, 16)
         return pltpu.make_async_remote_copy(
             src_ref=send_buf.at[pl.ds(start, size)],
             dst_ref=recv_buf.at[pl.ds(start, size)],
-            send_sem=fwd_send.at[p, q],
-            recv_sem=fwd_recv.at[p, q],
+            send_sem=fwd_send.at[stage, q],
+            recv_sem=fwd_recv.at[stage, q],
             device_id=pick(k, workers) if moved else workers[k],
             device_id_type=MESH,
         )
@@ -266,14 +286,45 @@
             device_id_type=MESH,
         )
 
-    for ks in ((0, 1), (2, 3)):
-        for p in range(2):
-            for k in ks:
-                forward(p, k, True).start()
+    def pieces(stage, quarters):
+        return [k for k in quarters if k % 2 == 0 or FWD_NARROW[stage]]
+
+    later = (z_me >= 4) & (z_me <= 6)
+
+    def send(stages, quarters):
+        for stage in stages:
+            for k in pieces(stage, quarters):
+                forward(stage, k, True).start()
+
+    send((0, 1), (0, 1))
+
+    @pl.when(jnp.logical_not(later))
+    def _():
+        send((2, 3), (0, 1))
+
+    send(range(4), (2, 3))
 
     for i in order:
         if i not in (0, 1, 9, 8):
             loads[i].wait()
+
+    row_on = pltpu.make_async_remote_copy(
+        src_ref=bias_table,
+        dst_ref=row_held,
+        send_sem=row_sem.at[0],
+        recv_sem=row_sem.at[1],
+        device_id=at(lon, two_on),
+        device_id_type=MESH,
+    )
+    row_own = pltpu.make_async_copy(bias_table, row_held, row_sem.at[2])
+
+    @pl.when(upper == 1)
+    def _():
+        row_on.start()
+
+    @pl.when(upper == 0)
+    def _():
+        row_own.start()
 
     w_qkv[0:D, :] = low(dot(qkv_weight[...], qkv_pad[...]))
     w_qkv[D:256, :] = jnp.zeros((256 - D, LANES), jnp.bfloat16)
@@ -290,19 +341,27 @@
 
     lane8 = lax.broadcasted_iota(jnp.int32, (8, 128), 1)
     row8 = lax.broadcasted_iota(jnp.int32, (8, 128), 0)
-    last = (lat == n_lat - 1).astype(jnp.int32)
+    last = (job_lat == n_lat - 1).astype(jnp.int32)
     query_half = (lax.rem(lane8, 8) >= 3).astype(jnp.int32)
     key_half = (row8 >= 3).astype(jnp.int32)
     left_out = (row8 >= WLAT).astype(jnp.int32) + last * (query_half ^ key_half) > 0
+
+    @pl.when(upper == 1)
+    def _():
+        row_on.wait_recv()
+
+    @pl.when(upper == 0)
+    def _():
+        row_own.wait()
 
     for p in range(2):
         table_pad[...] = jnp.zeros((8, WIDE), jnp.float32)
         if p == 0:
             for h in range(HEADS):
-                table_pad[h : h + 1, :] = bias_table[h, :, 0:WIDE]
+                table_pad[h : h + 1, :] = row_held[h, :, 0:WIDE]
         else:
             for h in range(HEADS):
-                table_pad[h : h + 1, 0 : REL - 2432] = bias_table[h, :, 2432:REL]
+                table_pad[h : h + 1, 0 : REL - 2432] = row_held[h, :, 2432:REL]
         entries = table_pad[...]
         for b in range(8):
             if b < WLAT:
@@ -325,16 +384,20 @@
                     block = near
                 bias[p, 8 * r : 8 * r + 8, 128 * h : 128 * h + 128] = jnp.where(left_out, MASKED, block)
 
+    @pl.when(later)
+    def _():
+        send((2, 3), (0, 1))
+
     gain_w, shift_w, query_w = vecs[0:1, :], vecs[1:2, :], vecs[2:3, :]
-    below64 = lax.broadcasted_iota(jnp.int32, (BOTH, 128), 1) < 64
+    below64 = lax.broadcasted_iota(jnp.int32, (WTOK, 128), 1) < 64
     low_lane = lax.broadcasted_iota(jnp.int32, (BOTH, 256), 1) < D
     flats = []
     kept = []
 
     def send_back(p):
-        per_window, normed, inverse = kept[p]
+        per_window = kept[p]
         rows = []
-        for w, (prob_low, score_low, key_w) in enumerate(per_window):
+        for w, (prob_low, score_low, key_w, _, _) in enumerate(per_window):
             value_g = dot(prob_low, u_heads[2 * p + w])
             key_g = dot(score_low, q_heads[2 * p + w]) * SCALE
             query_all = dot_tn(score_low, key_w)
@@ -343,6 +406,8 @@
                 term = query_all[h * 128 : h * 128 + WTOK] * head_mask[h : h + 1, :].astype(jnp.float32)
                 query_g = term if query_g is None else query_g + term
             rows.append(jnp.concatenate([low(query_g * SCALE), low(key_g), low(value_g)], 1))
+        normed = jnp.concatenate([window[3] for window in per_window], 0)
+        inverse = jnp.concatenate([window[4] for window in per_window], 0)
         hidden_grad = dot_nt(jnp.concatenate(rows, 0), w_qkv[...])
         scaled = hidden_grad * gain_w
         mean_g = jnp.sum(scaled, 1, keepdims=True) * (1.0 / D)
@@ -356,48 +421,50 @@
 
 
     for p in range(2):
-        for k in range(4):
-            forward(p, k, False).wait_recv()
-        got = [
-            recv_buf[pl.ds(FWD[k][0] + p * (FWD_CUT[k % 2] - 16), FWD_CUT[k % 2]), :] for k in range(4)
-        ]
-        tokens = dot(take_remote[pl.ds(3 * BOTH * p, 3 * BOTH), :], jnp.concatenate(got, 0))
-        x_a, x_b, x_c = tokens[0:BOTH], tokens[BOTH : 2 * BOTH], tokens[2 * BOTH :]
-        tail = jnp.where(below64, x_c, 0.0)
-        center = (jnp.sum(x_a, 1, keepdims=True) + jnp.sum(tail, 1, keepdims=True)) * (1.0 / D)
-        c_a = x_a - center
-        c_t = jnp.where(below64, x_c - center, 0.0)
-        spread_sq = (
-            jnp.sum(c_a * c_a, 1, keepdims=True) + jnp.sum(c_t * c_t, 1, keepdims=True)
-        ) * (1.0 / D)
-        inverse = lax.rsqrt(spread_sq + EPSILON)
-        normed = jnp.concatenate([c_a, c_t], 1) * inverse
-        hidden = low(normed * gain_w + shift_w)
-        projected = dot(hidden, w_qkv[...])
-        queries = low(projected[:, 0:256] + query_w)
-        keys = low(projected[:, 256:512])
-        values = low(projected[:, 512:768])
-        incoming = low(jnp.concatenate([x_b, x_c], 1))
-        upstream = low(dot_nt(incoming, w_proj[...]))
-
         per_window = []
         score_sum = None
         for w in range(2):
-            span = slice(w * WTOK, (w + 1) * WTOK)
-            q_w, u_w = q_heads.at[2 * p + w], u_heads.at[2 * p + w]
+            stage = 2 * p + w
+            for k in pieces(stage, range(4)):
+                forward(stage, k, False).wait_recv()
+            got = []
+            for k in range(4):
+                seen = (SEEN_NARROW if k % 2 else SEEN_WIDE)[stage]
+                if seen:
+                    got.append(recv_buf[pl.ds(FWD[k][0] + seen[0], seen[1]), :])
+            got = jnp.concatenate(got, 0)
+            rows = pl.ds(3 * WTOK * stage, 3 * WTOK)
+            tokens = dot(take_remote[rows, 0 : got.shape[0]], got)
+            x_a, x_b, x_c = tokens[0:WTOK], tokens[WTOK : 2 * WTOK], tokens[2 * WTOK :]
+            tail = jnp.where(below64, x_c, 0.0)
+            center = (jnp.sum(x_a, 1, keepdims=True) + jnp.sum(tail, 1, keepdims=True)) * (1.0 / D)
+            c_a = x_a - center
+            c_t = jnp.where(below64, x_c - center, 0.0)
+            spread_sq = (
+                jnp.sum(c_a * c_a, 1, keepdims=True) + jnp.sum(c_t * c_t, 1, keepdims=True)
+            ) * (1.0 / D)
+            inverse = lax.rsqrt(spread_sq + EPSILON)
+            normed = jnp.concatenate([c_a, c_t], 1) * inverse
+            hidden = low(normed * gain_w + shift_w)
+            projected = dot(hidden, w_qkv[...])
+            queries = low(projected[:, 0:256] + query_w)
+            keys = low(projected[:, 256:512])
+            values = low(projected[:, 512:768])
+            upstream = low(dot_nt(low(jnp.concatenate([x_b, x_c], 1)), w_proj[...]))
+            q_w, u_w = q_heads.at[stage], u_heads.at[stage]
             for h in range(HEADS):
                 mask = head_mask[h : h + 1, :]
-                q_w[pl.ds(h * 128, WTOK), :] = queries[span] * mask
-                u_w[pl.ds(h * 128, WTOK), :] = upstream[span] * mask
-            scores = dot_nt(keys[span], q_w[...]) * SCALE + bias[p]
+                q_w[pl.ds(h * 128, WTOK), :] = queries * mask
+                u_w[pl.ds(h * 128, WTOK), :] = upstream * mask
+            scores = dot_nt(keys, q_w[...]) * SCALE + bias[p]
             weights = jnp.exp(scores)
             probs = weights * (1.0 / jnp.sum(weights, 0, keepdims=True))
-            prob_grad = dot_nt(values[span], u_w[...])
+            prob_grad = dot_nt(values, u_w[...])
             inner = jnp.sum(probs * prob_grad, 0, keepdims=True)
             score_grad = probs * (prob_grad - inner)
             score_sum = score_grad if score_sum is None else score_sum + score_grad
-            per_window.append((low(probs), low(score_grad), keys[span]))
-        kept.append((per_window, normed, inverse))
+            per_window.append((low(probs), low(score_grad), keys, normed, inverse))
+        kept.append(per_window)
 
         for h in range(HEADS):
             near = far = None
@@ -477,20 +544,30 @@
         total = total + z_slots[z].astype(jnp.float32)
     final[...] = total
     own_slot = pltpu.make_async_copy(final, all_slots.at[plane_me], out_sem.at[2])
-    own_slot.start()
     gathered = []
-    for s in range(1, 8):
-        _, peer = plane_peer(s)
-        copy = pltpu.make_async_remote_copy(
-            src_ref=final,
-            dst_ref=all_slots.at[plane_me],
-            send_sem=all_send.at[s - 1],
-            recv_sem=all_recv.at[s - 1],
-            device_id=peer,
-            device_id_type=MESH,
+    for s in range(8):
+        rank = lax.rem(plane_me + s, 8)
+        peer = at(((rank // 2) * 8 + z_me) * 2 + lax.rem(rank, 2), job_lat if s else two_back)
+        gathered.append(
+            pltpu.make_async_remote_copy(
+                src_ref=final,
+                dst_ref=all_slots.at[plane_me],
+                send_sem=all_send.at[s],
+                recv_sem=all_recv.at[s],
+                device_id=peer,
+                device_id_type=MESH,
+            )
         )
+    for copy in gathered[1:]:
         copy.start()
-        gathered.append(copy)
+
+    @pl.when(upper == 1)
+    def _():
+        gathered[0].start()
+
+    @pl.when(upper == 0)
+    def _():
+        own_slot.start()
 
     written = []
     for p in range(2):
@@ -505,15 +582,30 @@
         copy.start()
         written.append(copy)
 
-    for copy in gathered:
-        copy.wait_recv()
-    for copy in written + [own_slot]:
-        copy.wait()
+    for stage in range(4):
+        for k in pieces(stage, range(4)):
+            forward(stage, k, False).wait_send()
     for p in range(2):
         for k in range(4):
-            forward(p, k, False).wait_send()
             backward(p, k, False).wait_send()
-    for copy in reduced + along + gathered:
+    for copy in reduced + along:
+        copy.wait_send()
+    for copy in written:
+        copy.wait()
+
+    @pl.when(upper == 1)
+    def _():
+        row_on.wait_send()
+        gathered[0].wait_recv()
+        gathered[0].wait_send()
+
+    @pl.when(upper == 0)
+    def _():
+        own_slot.wait()
+
+    for copy in gathered[1:]:
+        copy.wait_recv()
+    for copy in gathered[1:]:
         copy.wait_send()
 
 
@@ -579,16 +671,18 @@
         pltpu.VMEM((2 * TOK, D), bf16),
         dma((3,)),
         dma((len(args),)),
-        dma((2, 4)),
-        dma((2, 4)),
+        dma((4, 4)),
+        dma((4, 4)),
         dma((2, 4)),
         dma((2, 4)),
         dma((7,)),
         dma((7,)),
         dma((7,)),
         dma((7,)),
-        dma((7,)),
-        dma((7,)),
+        dma((8,)),
+        dma((8,)),
+        pltpu.VMEM((HEADS, 1, REL), f32),
+        dma((3,)),
         pltpu.SemaphoreType.REGULAR,
     ]
     grad, slots = pl.pallas_call(

time: 47.6 us -> 46.9 us (0.985)
  Pallas kernels: 46.8 us -> 46.1 us
    pallas_call x1, Pallas kernels: 45.1 us -> 44.5 us  [local(): pl.pallas_call(functools.partial(kernel, n_lon, n_lat, len(args)), out_sh...]
where the time goes in v4:
time: 46.9 us; the launch traced here: 46.8 us
  Pallas kernels  46.1 us (98%)
  between operations  0.64 us (1%)
    pallas_call x1, Pallas kernels, local(): pl.pallas_call(functools.partial(kernel, n_lon, n_lat, len(args)), out_sh...  44.5 us
    pallas_call x1, Pallas kernels, local(): pl.pallas_call(hand_over, out_shape=(jax.ShapeDtypeStruct((2 * TOK, D), b...  1.62 us

profile of v4, /device:TPU:1, one launch (start us, length us, event | category | flops | bytes accessed | tf_op | source)
XLA Modules:
  0.0 46.8 jit_solution(5155565567264481437)
XLA Ops:
  0.6 44.5 %shard_map.176 = (bf16[288,192]{1,0:T(8,128)(2,1)}, f32[8,16,128]{2,1,0:T(8,128)}) custom-call(bf16[288,192]{1,0:T(8,128)(2,1)} %bitcast.10, bf16[288,192]{1,0:T(8,128)(2,1)} %bitcast.11, f32[1,192]{1,0:T(1,128)} %bitcast.13, f32[1,192]{1,0:T(1,128)} %bitcast.14, bf16[192,576]{1,0:T(8,128)(2,1)} %refs_4_.1, f32[1,192]{1,0:T(1,128)} %bitcast.15, ...), custom_call_target="tpu_custom_call" | custom-call | tf_op jit(solution)/shard_map/pallas_call | solution.py:688
  45.1 1.6 %shard_map.177 = (bf16[288,192]{1,0:T(8,128)(2,1)}, f32[6,1,3312]{2,1,0:T(1,128)}) custom-call(bf16[288,192]{1,0:T(8,128)(2,1)} %get-tuple-element.6.grad, f32[8,16,128]{2,1,0:T(8,128)} %get-tuple-element.7.slots), custom_call_target="tpu_custom_call" | custom-call | tf_op jit(solution)/shard_map/pallas_call | solution.py:701

commit v5 on v4

--- a/solution.py
+++ b/solution.py
@@ -34,6 +34,7 @@
 LANES = HEADS * 128
 WIDE = 896
 MASKED = -1e30
+FAR_FIRST = (4, 3, 5, 2, 6, 7, 1)
 MESH = pl.DeviceIdType.MESH
 
 
@@ -499,7 +500,7 @@
     for c in range(8):
         red_src[c] = low(jnp.concatenate(tiles[2 * c : 2 * c + 2], 0))
     reduced = []
-    for s in range(1, 8):
+    for s in FAR_FIRST:
         rank, peer = plane_peer(s)
         copy = pltpu.make_async_remote_copy(
             src_ref=red_src.at[rank],
@@ -558,8 +559,8 @@
                 device_id_type=MESH,
             )
         )
-    for copy in gathered[1:]:
-        copy.start()
+    for s in FAR_FIRST:
+        gathered[s].start()
 
     @pl.when(upper == 1)
     def _():

time: 46.9 us -> 46.8 us (level)
  no operation moved by 1% of the time
where the time goes in v5:
time: 46.8 us; the launch traced here: 46.6 us
  Pallas kernels  45.9 us (98%)
  between operations  0.64 us (1%)
    pallas_call x1, Pallas kernels, local(): pl.pallas_call(functools.partial(kernel, n_lon, n_lat, len(args)), out_sh...  44.3 us
    pallas_call x1, Pallas kernels, local(): pl.pallas_call(hand_over, out_shape=(jax.ShapeDtypeStruct((2 * TOK, D), b...  1.62 us

profile of v5, /device:TPU:1, one launch (start us, length us, event | category | flops | bytes accessed | tf_op | source)
XLA Modules:
  0.0 46.6 jit_solution(8866505601197905284)
XLA Ops:
  0.6 44.3 %shard_map.176 = (bf16[288,192]{1,0:T(8,128)(2,1)}, f32[8,16,128]{2,1,0:T(8,128)}) custom-call(bf16[288,192]{1,0:T(8,128)(2,1)} %bitcast.10, bf16[288,192]{1,0:T(8,128)(2,1)} %bitcast.11, f32[1,192]{1,0:T(1,128)} %bitcast.13, f32[1,192]{1,0:T(1,128)} %bitcast.14, bf16[192,576]{1,0:T(8,128)(2,1)} %refs_4_.1, f32[1,192]{1,0:T(1,128)} %bitcast.15, ...), custom_call_target="tpu_custom_call" | custom-call | tf_op jit(solution)/shard_map/pallas_call | solution.py:689
  45.0 1.6 %shard_map.177 = (bf16[288,192]{1,0:T(8,128)(2,1)}, f32[6,1,3312]{2,1,0:T(1,128)}) custom-call(bf16[288,192]{1,0:T(8,128)(2,1)} %get-tuple-element.6.grad, f32[8,16,128]{2,1,0:T(8,128)} %get-tuple-element.7.slots), custom_call_target="tpu_custom_call" | custom-call | tf_op jit(solution)/shard_map/pallas_call | solution.py:702
